TPU v7x, 128 devices: a whole 4x4x4 slice. The times are simulated.
128 devices in a mesh: blk: 16 (over z_hi, y, core), hid: 8 (over x, z_lo).
Axes of the slice: x: 4, y: 4, z: 4 (z_hi: 2, z_lo: 2; z = z_hi * 2 + z_lo), core: 2. Of those that a mesh axis runs over, the one named last changes fastest.
Arguments:
- tokens: bfloat16 [8192, 1152], P('blk')
- cotangent: bfloat16 [8192, 1152], P('blk', 'hid'), may hold values from -6 to 6
- route_weight: float32 [8192, 2], P('blk'), may hold values from 0.1 to 1
- expert_ids: int32 [8192, 2], P('blk'), may hold values from 0 to 15, all different within a row; in each aligned block of 512 rows (0 to 511, 512 to 1023, ...) at most 128 rows name the same one
- timesteps: int32 [32], P('blk'), may hold values from 0 to 999
- time_table: float32 [1000, 1152], replicated, may hold values from -6 to 6
- up_weight: bfloat16 [16, 1152, 4608], P('blk', None, 'hid'), may hold values from -0.25 to 0.25
- down_weight: bfloat16 [16, 4608, 1152], P('blk', 'hid'), may hold values from -0.125 to 0.125
- modulation_weight: float32 [1152, 3, 1152], P(None, None, 'hid'), may hold values from -0.1875 to 0.1875
- modulation_bias: float32 [3, 1152], P(None, 'hid'), may hold values from -3 to 3
Outputs:
- token_grads: bfloat16 [8192, 1152], P('blk', 'hid')
- up_grads: float32 [16, 1152, 4608], P('blk', None, 'hid')
- down_grads: float32 [16, 4608, 1152], P('blk', 'hid')
- modulation_weight_grads: float32 [1152, 3, 1152], P('blk', None, 'hid')
- modulation_bias_grads: float32 [3, 1152], P(None, 'hid')
Inputs may be any that keep to these rules, and one draw needn't show every extreme that they name: `expert_ids`: each row names 2 different experts. In the rows of one index of blk (aligned blocks of 512 tokens) no expert is named more than 128 times, and in every draw some expert is named exactly 128 times in some block.
All inputs are finite; a program needn't handle non-finite values.
Results may differ from a plain program's by a relative error of at most 0.023.
Values may be sent and summed in bfloat16 or wider, within the bound.
A program may use at most 128 MiB of HBM per device.

v0:
```python
import math

import jax
import jax.numpy as jnp
from jax import lax
from jax.sharding import PartitionSpec as P

norm_epsilon = 1e-06
gelu_cubic = 0.044715
gelu_factor = math.sqrt(2.0 / math.pi)


def gelu_tanh(values):
    inner = gelu_factor * (values + gelu_cubic * values * values * values)
    return 0.5 * values * (1.0 + jnp.tanh(inner))


def gelu_slope(values):
    inner = gelu_factor * (values + gelu_cubic * values * values * values)
    tangent = jnp.tanh(inner)
    return 0.5 * (1.0 + tangent) + 0.5 * values * (1.0 - tangent * tangent) * gelu_factor * (
        1.0 + 3.0 * gelu_cubic * values * values
    )


def on_device(
    tokens,
    cotangent,
    route_weight,
    expert_ids,
    timesteps,
    time_table,
    up_weight,
    down_weight,
    modulation_weight,
    modulation_bias,
):
    tok_count, width = tokens.shape
    narrow = cotangent.shape[1]
    blk_count = lax.axis_size("blk")
    column_first = lax.axis_index("hid") * narrow
    image_count = timesteps.shape[0]
    per_image = tok_count // image_count
    choices_each = route_weight.shape[1]
    capacity = 2 * choices_each * tok_count // blk_count
    slot_total = blk_count * capacity
    pair_total = tok_count * choices_each
    lookup = (
        timesteps[:, None] == jnp.arange(time_table.shape[0], dtype=jnp.int32)[None, :]
    ).astype(jnp.float32)
    condition = jax.nn.silu(
        jnp.dot(
            lookup, time_table, precision=lax.Precision.HIGHEST, preferred_element_type=jnp.float32
        )
    )
    mod_part = (
        jnp.einsum("bi,icd->bcd", condition, modulation_weight, precision=lax.Precision.HIGHEST)
        + modulation_bias[None]
    )
    mod_full = lax.all_gather(mod_part, "hid", axis=2, tiled=True)
    full_tok = jnp.repeat(mod_full, per_image, axis=0)
    own_tok = jnp.repeat(mod_part, per_image, axis=0)
    inputs = tokens.astype(jnp.float32)
    row_mean = jnp.mean(inputs, axis=1, keepdims=True)
    spread = jnp.mean((inputs - row_mean) ** 2, axis=1, keepdims=True)
    inv_spread = 1.0 / jnp.sqrt(spread + norm_epsilon)
    normed = (inputs - row_mean) * inv_spread
    expert_in = (normed * (1.0 + full_tok[:, 1]) + full_tok[:, 0]).astype(jnp.bfloat16)
    grad_out = cotangent.astype(jnp.float32)
    pair_ids = expert_ids.reshape(pair_total)
    one_hot = (pair_ids[:, None] == jnp.arange(blk_count, dtype=jnp.int32)[None, :]).astype(
        jnp.int32
    )
    before = jnp.cumsum(one_hot, axis=0) - one_hot
    slot = jnp.sum(one_hot * before, axis=1)
    target = pair_ids * capacity + slot
    matches = target[None, :] == jnp.arange(slot_total, dtype=jnp.int32)[:, None]
    source_pair = jnp.sum(
        jnp.where(matches, jnp.arange(pair_total, dtype=jnp.int32)[None, :], 0), axis=1
    )
    occupied = jnp.any(matches, axis=1)[:, None]
    token_of_slot = source_pair // choices_each
    weight_of_slot = jnp.take(route_weight.reshape(pair_total), source_pair)[:, None]
    send_in = jnp.where(
        occupied, jnp.take(expert_in, token_of_slot, axis=0), jnp.zeros((), jnp.bfloat16)
    )
    full_cot = lax.all_gather(cotangent, "hid", axis=1, tiled=True)
    gated_full = full_tok[:, 2] * full_cot.astype(jnp.float32)
    send_cot = jnp.where(
        occupied, weight_of_slot * jnp.take(gated_full, token_of_slot, axis=0), 0.0
    ).astype(jnp.bfloat16)
    recv_in, recv_cot = (
        lax.all_to_all(
            send_in.reshape(blk_count, capacity, width),
            "blk",
            split_axis=0,
            concat_axis=0,
            tiled=True,
        ),
        lax.all_to_all(
            send_cot.reshape(blk_count, capacity, width),
            "blk",
            split_axis=0,
            concat_axis=0,
            tiled=True,
        ),
    )
    rows_in = recv_in.reshape(slot_total, width)
    rows_cot = recv_cot.reshape(slot_total, width)
    up_matrix = up_weight[0]
    down_matrix = down_weight[0]
    pre_act = jnp.dot(rows_in, up_matrix, preferred_element_type=jnp.float32)
    activated = gelu_tanh(pre_act).astype(jnp.bfloat16)
    act_grad = lax.dot_general(
        rows_cot, down_matrix, (((1,), (1,)), ((), ())), preferred_element_type=jnp.float32
    )
    pre_grad = (act_grad * gelu_slope(pre_act)).astype(jnp.bfloat16)
    up_grads = lax.dot_general(
        rows_in, pre_grad, (((0,), (0,)), ((), ())), preferred_element_type=jnp.float32
    )[None]
    down_grads = lax.dot_general(
        activated, rows_cot, (((0,), (0,)), ((), ())), preferred_element_type=jnp.float32
    )[None]
    out_rows = lax.dot_general(
        down_matrix, activated, (((0,), (1,)), ((), ())), preferred_element_type=jnp.float32
    )
    grad_rows = lax.dot_general(
        up_matrix, pre_grad, (((1,), (1,)), ((), ())), preferred_element_type=jnp.float32
    )
    summed = lax.psum_scatter(
        jnp.stack([out_rows, grad_rows], axis=1).astype(jnp.bfloat16),
        "hid",
        scatter_dimension=0,
        tiled=True,
    ).astype(jnp.float32)
    returned = lax.all_to_all(
        summed.astype(jnp.bfloat16), "blk", split_axis=2, concat_axis=2, tiled=True
    ).astype(summed.dtype)
    picked = jnp.take(returned, target, axis=2)
    out_pairs = picked[:, 0].reshape(narrow, tok_count, choices_each)
    grad_pairs = picked[:, 1].reshape(narrow, tok_count, choices_each)
    moe = jnp.sum(route_weight[None] * out_pairs, axis=2).T
    mixed_grad = jnp.sum(grad_pairs, axis=2).T
    normed_own = lax.dynamic_slice_in_dim(normed, column_first, narrow, 1)
    shift_grad = jnp.sum(mixed_grad.reshape(image_count, per_image, narrow), axis=1)
    scale_grad = jnp.sum((mixed_grad * normed_own).reshape(image_count, per_image, narrow), axis=1)
    gate_grad = jnp.sum((grad_out * moe).reshape(image_count, per_image, narrow), axis=1)
    modulation_grads = jnp.stack([shift_grad, scale_grad, gate_grad], axis=1)
    norm_grad = mixed_grad * (1.0 + own_tok[:, 1])
    first_sum, second_sum = lax.psum(
        (jnp.sum(norm_grad, axis=1), jnp.sum(norm_grad * normed_own, axis=1)), "hid"
    )
    first_mean = (first_sum / width)[:, None]
    second_mean = (second_sum / width)[:, None]
    token_grads = (
        grad_out + inv_spread * (norm_grad - first_mean - normed_own * second_mean)
    ).astype(jnp.bfloat16)
    modulation_weight_grads = lax.psum_scatter(
        jnp.einsum(
            "bi,bcd->icd", condition, modulation_grads, precision=lax.Precision.HIGHEST
        ).astype(jnp.bfloat16),
        "blk",
        scatter_dimension=0,
        tiled=True,
    ).astype(jnp.float32)
    modulation_bias_grads = lax.psum(jnp.sum(modulation_grads, axis=0), "blk")
    return (token_grads, up_grads, down_grads, modulation_weight_grads, modulation_bias_grads)


def solution(mesh):
    in_specs = (
        P("blk", None),
        P("blk", "hid"),
        P("blk", None),
        P("blk", None),
        P("blk"),
        P(),
        P("blk", None, "hid"),
        P("blk", "hid", None),
        P(None, None, "hid"),
        P(None, "hid"),
    )
    out_specs = (
        P("blk", "hid"),
        P("blk", None, "hid"),
        P("blk", "hid", None),
        P("blk", None, "hid"),
        P(None, "hid"),
    )
    return jax.shard_map(
        on_device, mesh=mesh, in_specs=in_specs, out_specs=out_specs, check_vma=False
    )
```

profile of v0, /device:TPU:1, one launch (start us, length us, event | category | flops | bytes accessed | tf_op | source)
XLA Modules:
  0.0 834.2 jit_solution(3973286924959632668)
XLA Ops:
  10.6 4.0 divide_multiply_fusion
  16.7 4.5 reduce-window.6
  21.6 47.3 %all_gather.6 = f32[2,3,1152]{1,0,2:T(2,128)S(1)} all-gather(f32[2,3,144]{1,0,2:T(2,128)S(1)} %copy.51), channel_id=1, replica_groups=mesh['blk'=16,'hid'=8] {'hid'}, dimensions={2}, use_global_device_ids=true | all-gather | bytes 31104 | tf_op jit(solution)/shard_map/all_gather | solution.py:60
  79.7 3.3 fusion.13
  83.0 10.4 %gather_fusion = bf16[2048,1152]{1,0:T(8,128)(2,1)} fusion(bf16[512,1152]{1,0:T(8,128)(2,1)S(1)} %get-tuple-element.36, s32[2048]{0:T(1024)} %broadcast_clamp_fusion.1), kind=kCustom, calls=%fused_computation | custom fusion | bytes 9445376 | tf_op jit(solution)/shard_map/jit(_take)/gather | solution.py:85
  93.4 4.4 select_select_fusion
  97.8 9.3 %all-to-all-start = ((bf16[16,128,1152]{2,1,0:T(8,128)(2,1)}), bf16[16,128,1152]{2,1,0:T(8,128)(2,1)}, u32[]{:S(2)}, u32[]{:S(2)}) async-start(bf16[16,128,1152]{2,1,0:T(8,128)(2,1)} %select_select_fusion), calls=%async_computation | async-start | bytes 9437184 | tf_op jit(solution)/shard_map/all_to_all | solution.py:93
  107.6 8.6 %gather_fusion.1 = f32[2048]{0:T(1024)S(1)} fusion(f32[1024]{0:T(1024)S(1)} %reshape.243, s32[2048]{0:T(1024)S(1)} %broadcast_clamp_fusion), kind=kCustom, calls=%fused_computation.1 | custom fusion | bytes 24576 | tf_op jit(solution)/shard_map/jit(_take)/gather | solution.py:83
  116.2 10.4 %gather_fusion.2 = f32[2048,1152]{1,0:T(8,128)} fusion(f32[512,1152]{1,0:T(8,128)S(1)} %get-tuple-element.35, s32[2048]{0:T(1024)S(1)} %copy-done.7), kind=kCustom, calls=%fused_computation.2 | custom fusion | bytes 18882560 | tf_op jit(solution)/shard_map/jit(_take)/gather | solution.py:90
  126.6 6.0 select_convert_fusion
  132.5 37.7 %all-to-all-done = bf16[16,128,1152]{2,1,0:T(8,128)(2,1)} async-done(((bf16[16,128,1152]{2,1,0:T(8,128)(2,1)}), bf16[16,128,1152]{2,1,0:T(8,128)(2,1)}, u32[]{:S(2)}, u32[]{:S(2)}) %all-to-all-start) | async-done | bytes 4718624 | tf_op jit(solution)/shard_map/all_to_all | solution.py:93
  170.3 6.4 all-to-all-start.1
  177.2 5.2 fusion.21
  184.6 6.3 fusion.1
  190.9 48.9 %all-to-all-done.1 = bf16[16,128,1152]{2,1,0:T(8,128)(2,1)} async-done(((bf16[16,128,1152]{2,1,0:T(8,128)(2,1)}), bf16[16,128,1152]{2,1,0:T(8,128)(2,1)}, u32[]{:S(2)}, u32[]{:S(2)}) %all-to-all-start.1) | async-done | bytes 4718624 | tf_op jit(solution)/shard_map/all_to_all | solution.py:100
  239.8 8.3 fusion.9
  249.5 5.8 fusion.2
  255.3 8.3 %pad_maximum_fusion = bf16[1152,2,2048]{0,2,1:T(8,128)(2,1)} fusion(bf16[1152,1,2048]{0,2,1:T(8,128)(2,1)} %fusion.2, bf16[1152,1,2048]{0,2,1:T(8,128)(2,1)} %fusion.1), kind=kLoop, calls=%fused_computation.4 | loop fusion | flops 4718592 | bytes 18874368 | tf_op jit(solution)/shard_map/stack | solution.py:131
  263.7 24.0 %copy.55 = bf16[1152,2,2048]{2,1,0:T(2,128)(2,1)} copy(bf16[1152,2,2048]{0,2,1:T(8,128)(2,1)} %pad_maximum_fusion) | data formatting | bytes 18874368 | tf_op jit(solution)/shard_map/stack | solution.py:131
  289.6 375.6 %all-reduce.4.cloned.1.call-done = bf16[1152,2,2048]{2,1,0:T(2,128)(2,1)} async-done(((bf16[1152,2,2048]{2,1,0:T(2,128)(2,1)}), bf16[1152,2,2048]{2,1,0:T(2,128)(2,1)}) %all-reduce.4.cloned.1.call-update) | async-done | bytes 9437200
  667.4 6.0 copy.56
  673.3 7.3 all-to-all-start.2
  681.9 27.3 %all-to-all-done.2 = bf16[144,2,2048]{0,1,2:T(2,128)(2,1)S(1)} async-done(((bf16[144,2,2048]{0,1,2:T(2,128)(2,1)}), bf16[144,2,2048]{0,1,2:T(2,128)(2,1)S(1)}, u32[]{:S(2)}, u32[]{:S(2)}) %all-to-all-start.2) | async-done | bytes 1179680 | tf_op jit(solution)/shard_map/all_to_all | solution.py:136
  709.2 3.3 convert_element_type.54
  712.5 6.3 gather_fusion.3
  718.8 3.7 select_bitcast_fusion
  722.5 5.6 slice_reduce_fusion
  738.9 9.3 %copy.60 = bf16[1152,3,144]{2,1,0:T(4,128)(2,1)S(1)} copy(bf16[1152,3,144]{2,0,1:T(8,128)(2,1)S(1)} %convolution_convert_fusion.2) | data formatting | bytes 1990656
  750.6 9.5 %convolution_bitcast_fusion.1 = f32[1,576,1152]{2,1,0:T(8,128)} fusion(bf16[2048,1152]{1,0:T(8,128)(2,1)} %bitcast.20, f32[2048,576]{0,1:T(8,128)} %copy-done.28), kind=kOutput, calls=%fused_computation.26 | convolution fusion | flops 2728525824 | bytes 12091392 | tf_op jit(solution)/shard_map/dot_general | solution.py:121
  760.1 7.2 convolution_bitcast_fusion
  770.1 15.8 %all-reduce.1 = (f32[512]{0:T(512)S(1)}, f32[512]{0:T(512)S(1)}) all-reduce(f32[512]{0:T(512)S(1)} %get-tuple-element.28, f32[512]{0:T(512)S(1)} %get-tuple-element.27), channel_id=1, replica_groups=mesh['blk'=16,'hid'=8] {'hid'}, use_global_device_ids=true, to_apply=%region_12.13 | all-reduce | flops 1024 | bytes 8192 | tf_op jit(solution)/shard_map/psum | solution.py:150
  788.7 37.0 %psum.23 = f32[3,144]{1,0:T(4,128)} all-reduce(f32[3,144]{1,0:T(4,128)S(1)} %fusion.41), channel_id=1, replica_groups=mesh['blk'=16,'hid'=8] {'blk'}, use_global_device_ids=true, to_apply=%region_19.20 | all-reduce | flops 432 | bytes 3456 | tf_op jit(solution)/shard_map/psum | solution.py:166
  (124 shorter events, 45.8 us)
Async XLA Ops:
  7.2 7.5 copy-start
  7.2 7.4 copy-start.22
  7.2 68.8 %all-gather.2.cloned.1.call-start = ((), (), s32[]{:S(2)}) async-start(), calls=%async_computation.4 | async-start | bytes 1327104 | tf_op jit(solution)/shard_map/all_gather | solution.py:87
  10.6 59.4 %copy-start.15 = (f32[512]{0:T(512)}, f32[512]{0:T(512)S(1)}, u32[]{:S(2)}) copy-start(f32[512]{0:T(512)S(1)} %broadcast_multiply_fusion.3) | copy-start | bytes 6148
  10.6 59.4 %copy-start.2 = (bf16[512,1152]{1,0:T(8,128)(2,1)S(1)}, bf16[512,1152]{1,0:T(8,128)(2,1)}, u32[]{:S(2)}) copy-start(bf16[512,1152]{1,0:T(8,128)(2,1)} %param.10) | copy-start | bytes 3538948
  16.5 62.4 %copy-start.10 = (f32[2,3,144]{2,0,1:T(2,128)}, f32[2,3,144]{2,0,1:T(2,128)S(1)}, u32[]{:S(2)}) copy-start(f32[2,3,144]{2,0,1:T(2,128)S(1)} %convolution_add_fusion) | copy-start | bytes 10372
  70.0 2.7 copy-start.12
  74.2 4.7 copy-start.8
  76.0 2.9 copy-start.16
  83.0 10.4 %copy-start.18 = (pred[16,128]{1,0:T(8,128)(4,1)S(1)}, pred[16,128]{1,0:T(8,128)(4,1)}, u32[]{:S(2)}) copy-start(pred[16,128]{1,0:T(8,128)(4,1)} %compare_and_fusion) | copy-start | bytes 6148
  97.8 9.4 %copy-start.23 = (f32[512,2]{0,1:T(2,128)S(1)}, f32[512,2]{0,1:T(2,128)}, u32[]{:S(2)}) copy-start(f32[512,2]{0,1:T(2,128)} %param.12) | copy-start | bytes 12292
  97.8 9.7 %copy-start.14 = (s32[2048,1]{0,1:T(1,128)S(1)}, s32[2048,1]{0,1:T(1,128)}, u32[]{:S(2)}) copy-start(s32[2048,1]{0,1:T(1,128)} %get-tuple-element.38) | copy-start | bytes 24580
  97.8 72.4 %all-to-all-start = ((bf16[16,128,1152]{2,1,0:T(8,128)(2,1)}), bf16[16,128,1152]{2,1,0:T(8,128)(2,1)}, u32[]{:S(2)}, u32[]{:S(2)}) async-start(bf16[16,128,1152]{2,1,0:T(8,128)(2,1)} %select_select_fusion), calls=%async_computation | async-start | bytes 9437184 | tf_op jit(solution)/shard_map/all_to_all | solution.py:93
  107.2 9.0 %copy-start.9 = (s32[2048]{0:T(1024)S(1)}, s32[2048]{0:T(1024)}, u32[]{:S(2)}) copy-start(s32[2048]{0:T(1024)} %copy-done.8) | copy-start | bytes 24580
  107.2 9.0 %copy-start.7 = (s32[2048]{0:T(1024)S(1)}, s32[2048]{0:T(1024)}, u32[]{:S(2)}) copy-start(s32[2048]{0:T(1024)} %broadcast_clamp_fusion.1) | copy-start | bytes 24580
  116.2 10.4 %copy-start.19 = (pred[16,128]{1,0:T(8,128)(4,1)S(1)}, pred[16,128]{1,0:T(8,128)(4,1)}, u32[]{:S(2)}) copy-start(pred[16,128]{1,0:T(8,128)(4,1)} %compare_and_fusion) | copy-start | bytes 6148
  116.2 10.4 %copy-start.21 = (pred[2048]{0:T(1024)(128)(4,1)S(1)}, pred[2048]{0:T(1024)(128)(4,1)}, u32[]{:S(2)}) copy-start(pred[2048]{0:T(1024)(128)(4,1)} %fusion) | copy-start | bytes 6148
  132.5 44.7 %copy-start.26 = (bf16[1,1152,576]{1,2,0:T(8,128)(2,1)S(1)}, bf16[1,1152,576]{1,2,0:T(8,128)(2,1)}, u32[]{:S(2)}) copy-start(bf16[1,1152,576]{1,2,0:T(8,128)(2,1)} %param.16) | copy-start | bytes 3981316
  170.3 69.5 %all-to-all-start.1 = ((bf16[16,128,1152]{2,1,0:T(8,128)(2,1)}), bf16[16,128,1152]{2,1,0:T(8,128)(2,1)}, u32[]{:S(2)}, u32[]{:S(2)}) async-start(bf16[16,128,1152]{2,1,0:T(8,128)(2,1)} %select_convert_fusion), calls=%async_computation.1 | async-start | bytes 9437184 | tf_op jit(solution)/shard_map/all_to_all | solution.py:100
  176.7 488.6 %all-reduce.4.cloned.1.call-start = ((), (), s32[]{:S(2)}) async-start(), calls=%async_computation.6 | async-start | bytes 18874368
  177.2 7.4 copy-start.25
  289.6 391.0 %copy-start.6 = (bf16[512,144]{0,1:T(8,128)(2,1)S(1)}, bf16[512,144]{0,1:T(8,128)(2,1)}, u32[]{:S(2)}) copy-start(bf16[512,144]{0,1:T(8,128)(2,1)} %param.11) | copy-start | bytes 442372
  289.6 391.9 %copy-start.20 = (s32[512,2]{0,1:T(2,128)S(1)}, s32[512,2]{0,1:T(2,128)}, u32[]{:S(2)}) copy-start(s32[512,2]{0,1:T(2,128)} %param.13) | copy-start | bytes 12292
  667.3 14.5 %copy-start.13 = (s32[1024]{0:T(1024)S(1)}, s32[1024]{0:T(1024)}, u32[]{:S(2)}) copy-start(s32[1024]{0:T(1024)} %copy-done.12) | copy-start | bytes 12292
  673.3 35.9 %all-to-all-start.2 = ((bf16[144,2,2048]{0,1,2:T(2,128)(2,1)}), bf16[144,2,2048]{0,1,2:T(2,128)(2,1)S(1)}, u32[]{:S(2)}, u32[]{:S(2)}) async-start(bf16[144,2,2048]{0,1,2:T(2,128)(2,1)} %copy.56), calls=%async_computation.2 | async-start | bytes 4194304 | tf_op jit(solution)/shard_map/all_to_all | solution.py:136
  680.6 145.1 %reduce-scatter.4.cloned.1.call-start = ((), (), s32[]{:S(2)}) async-start(), calls=%async_computation.5 | async-start | bytes 1253376
  681.5 37.3 %copy-start.24 = (pred[1024]{0:T(1024)(128)(4,1)S(1)}, pred[1024]{0:T(1024)(128)(4,1)}, u32[]{:S(2)}) copy-start(pred[1024]{0:T(1024)(128)(4,1)} %get-tuple-element.33) | copy-start | bytes 3076
  750.6 9.5 %copy-start.30 = (bf16[2048,576]{0,1:T(8,128)(2,1)S(1)}, bf16[2048,576]{0,1:T(8,128)(2,1)}, u32[]{:S(2)}) copy-start(bf16[2048,576]{0,1:T(8,128)(2,1)} %copy-done.29) | copy-start | bytes 7077892
  760.1 7.2 copy-start.11
  760.1 25.9 %copy-start.5 = (bf16[512,144]{1,0:T(8,128)(2,1)S(1)}, bf16[512,144]{1,0:T(8,128)(2,1)}, u32[]{:S(2)}) copy-start(bf16[512,144]{1,0:T(8,128)(2,1)} %copy.46) | copy-start | bytes 442372
  760.1 25.9 %copy-start.17 = (f32[512]{0:T(512)S(1)}, f32[512]{0:T(512)}, u32[]{:S(2)}) copy-start(f32[512]{0:T(512)} %add_rsqrt_fusion) | copy-start | bytes 6148
  760.1 67.3 %copy-start.1 = (f32[1152,3,144]{0,2,1:T(8,128)S(1)}, f32[1152,3,144]{0,2,1:T(8,128)}, u32[]{:S(2)}) copy-start(f32[1152,3,144]{0,2,1:T(8,128)} %param.18) | copy-start | bytes 5971972
  (5 other events, 6.6 us)
Sparse Core Ops, SparseCore 0:
  9.7 55.3 all-gather.1
  287.9 377.3 all-reduce.3
  750.7 68.9 reduce-scatter.3
where the time goes:
time: 844 us; the launch traced here: 834 us
  waiting for transfers between devices  490 us (58%)
  local copies, waits for them, and re-layouts  102 us (12%)
  blocking collectives  100 us (12%)
  other arithmetic  51.8 us (6%)
  matrix products  51.2 us (6%)
  starting transfers between devices  23.6 us (3%)
  between operations  15.2 us (2%)
    unnamed x5, waiting for transfers between devices  376 us
    all_to_all x1, waiting for transfers between devices, on_device(): lax.all_to_all(send_cot.reshape(blk_count, capacity, width), 'blk', split...  48.9 us
    all_gather x1, blocking collectives, on_device(): mod_full = lax.all_gather(mod_part, 'hid', axis=2, tiled=True)  47.3 us
    all_to_all x1, waiting for transfers between devices, on_device(): lax.all_to_all(send_in.reshape(blk_count, capacity, width), 'blk', split_...  37.7 us
    psum x1, blocking collectives, on_device(): modulation_bias_grads = lax.psum(jnp.sum(modulation_grads, axis=0), 'blk')  37 us
    all_to_all x1, waiting for transfers between devices, on_device(): lax.all_to_all(summed.astype(jnp.bfloat16), 'blk', split_axis=2, concat_a...  27.3 us
    unnamed x71, local copies, waits for them, and re-layouts  24.2 us
    another operation x1, local copies, waits for them, and re-layouts, on_device(): jnp.stack([out_rows, grad_rows], axis=1).astype(jnp.bfloat16)  24 us
  transfers between devices with their start and end apart: 6, of which 4 were waited for; matrix products, arithmetic and copies ran while one was open for 10% of the time, Pallas kernels for 0%

commit v1 on v0

v1 whole, which is shorter than its diff:
```python
import math

import jax
import jax.numpy as jnp
from jax import lax
from jax.experimental import pallas as pl
from jax.experimental.pallas import tpu as pltpu
from jax.sharding import PartitionSpec as P

MESH = pl.DeviceIdType.MESH
norm_epsilon = 1e-06
gelu_cubic = 0.044715
gelu_factor = math.sqrt(2.0 / math.pi)

N_BLK, N_HID = 16, 8
WIDTH, NARROW, CAP = 1152, 144, 128
SLOTS = N_BLK * CAP
GROUPS = 4
LANES = SLOTS // GROUPS
HALF = LANES // 2
ORDER = (0, 1, 6, 2, 7, 3, 5, 4)


def shift(j):
    return j // 8, ORDER[j % 8]


class Place:
    def __init__(self):
        self.blk = lax.axis_index("blk")
        self.hid = lax.axis_index("hid")
        self.z_hi, self.m = self.blk // 8, self.blk % 8
        self.x, self.z_lo = self.hid // 2, self.hid % 2
        self.x_right, self.x_left, self.x_far = [(self.x + i) % 4 for i in (1, 3, 2)]
        self.right = (self.blk, self.x_right * 2 + self.z_lo)
        self.left = (self.blk, self.x_left * 2 + self.z_lo)
        self.across = (self.blk, self.home(1))

    def home(self, a):
        return self.hid if a == 0 else self.hid + 1 - 2 * self.z_lo

    def later(self, j):
        a, m = shift(j)
        return (self.z_hi + a) % 2 * 8 + (self.m + m) % 8

    def earlier(self, j):
        a, m = shift(j)
        return (self.z_hi + a) % 2 * 8 + (self.m + 8 - m) % 8

    def hid_peer(self, i):
        return (self.blk, (self.hid + i) % 8)


def greet(devices):
    barrier = pltpu.get_barrier_semaphore()
    for device in devices:
        pl.semaphore_signal(barrier, inc=1, device_id=device, device_id_type=MESH)
    pl.semaphore_wait(barrier, len(devices))


def send(src, dst, send_sem, recv_sem, device, sent):
    copy = pltpu.make_async_remote_copy(
        src_ref=src, dst_ref=dst, send_sem=send_sem, recv_sem=recv_sem, device_id=device, device_id_type=MESH
    )
    copy.start()
    sent.append(copy)


def arrived(region, send_sem, recv_sem, device):
    pltpu.make_async_remote_copy(
        src_ref=region, dst_ref=region, send_sem=send_sem, recv_sem=recv_sem, device_id=device, device_id_type=MESH
    ).wait_recv()


def rows_of(slice_index, count=1):
    return pl.ds(pl.multiple_of(slice_index * NARROW, 16), count * NARROW)


def block_of(index):
    return pl.ds(pl.multiple_of(index * CAP, CAP), CAP)


def dispatch_kernel(
    px, pc, info, xt, ct, table, a2a_send, a2a_recv, ring_send, ring_recv, info_send, info_recv, local_sem
):
    at = Place()
    peers = [(at.later(j), at.home(j // 8)) for j in range(N_BLK)]
    greet(peers[1:] + [at.hid_peer(i) for i in range(1, N_HID)])
    own = rows_of(at.hid)
    sent = []
    local = []
    for j in range(N_BLK):
        lanes = pl.ds(j * CAP, CAP)
        target = at.later(j)
        parts = (
            (px.at[:, block_of(target)], xt.at[own, lanes]),
            (pc.at[:, block_of(target)], ct.at[own, lanes]),
            (info.at[target], table.at[at.hid, j]),
        )
        for i, (src, dst) in enumerate(parts):
            if j == 0:
                copy = pltpu.make_async_copy(src, dst, local_sem.at[i])
                copy.start()
                local.append(copy)
            else:
                send(src, dst, a2a_send.at[j, i], a2a_recv.at[j, i], peers[j], sent)

    def from_peer(j, i, region):
        if j == 0:
            local[i].wait()
        else:
            arrived(region, a2a_send.at[j, i], a2a_recv.at[j, i], peers[j])

    def ring(g):
        a = g // (GROUPS // 2)
        f = at.home(a)
        other = at.home(1 - a)
        zf = f % 2
        lanes = pl.ds(g * LANES, LANES)
        halves = [pl.ds(g * LANES + i * HALF, HALF) for i in range(2)]
        far_slice = at.x_far * 2 + zf

        def go(array, rows, cols, k, device):
            region = array.at[rows, cols]
            send(region, region, ring_send.at[g, k], ring_recv.at[g, k], device, sent)

        def come(array, rows, cols, k):
            arrived(array.at[rows, cols], ring_send.at[g, k], ring_recv.at[g, k], at.across)

        def first():
            for j in range(g * LANES // CAP, (g + 1) * LANES // CAP):
                from_peer(j, 0, xt.at[rows_of(f), pl.ds(j * CAP, CAP)])
                from_peer(j, 1, ct.at[rows_of(f), pl.ds(j * CAP, CAP)])
            go(xt, rows_of(f), lanes, 0, at.across)
            go(ct, rows_of(f), lanes, 6, at.right)
            go(ct, rows_of(f), lanes, 7, at.left)
            go(ct, rows_of(f), lanes, 5, at.across)

        def second():
            come(xt, rows_of(other), lanes, 0)
            go(xt, rows_of(at.x * 2, 2), lanes, 1, at.right)
            go(xt, rows_of(at.x * 2, 2), lanes, 2, at.left)
            left, right = rows_of(at.x_left * 2 + zf), rows_of(at.x_right * 2 + zf)
            come(ct, left, lanes, 6)
            go(ct, left, halves[0], 8, at.right)
            go(ct, left, lanes, 10, at.across)
            come(ct, right, lanes, 7)
            go(ct, right, halves[1], 9, at.left)
            go(ct, right, lanes, 11, at.across)

        def third():
            come(xt, rows_of(at.x_left * 2, 2), lanes, 1)
            go(xt, rows_of(at.x_left * 2), lanes, 3, at.right)
            come(xt, rows_of(at.x_right * 2, 2), lanes, 2)
            go(xt, rows_of(at.x_right * 2 + 1), lanes, 4, at.left)
            for i in range(2):
                come(ct, rows_of(far_slice), halves[i], 8 + i)
                go(ct, rows_of(far_slice), halves[i], 12 + i, at.across)

        def fourth():
            come(xt, rows_of(at.x_far * 2), lanes, 3)
            come(xt, rows_of(at.x_far * 2 + 1), lanes, 4)
            come(ct, rows_of(other), lanes, 5)
            come(ct, rows_of(at.x_left * 2 + 1 - zf), lanes, 10)
            come(ct, rows_of(at.x_right * 2 + 1 - zf), lanes, 11)
            for i in range(2):
                come(ct, rows_of(at.x_far * 2 + 1 - zf), halves[i], 12 + i)

        return first, second, third, fourth

    steps = [ring(g) for g in range(GROUPS)]

    def spread_info():
        for a in range(2):
            f = at.home(a)
            for j in range(8 * a, 8 * a + 8):
                from_peer(j, 2, table.at[f, j])
            half = table.at[f, pl.ds(8 * a, 8)]
            for i in range(1, N_HID):
                send(half, half, info_send.at[a, i], info_recv.at[a, i], at.hid_peer(i), sent)

    def gather_info():
        for a in range(2):
            for i in range(1, N_HID):
                q = (at.hid + 8 - i) % 8
                f = q if a == 0 else q + 1 - 2 * (q % 2)
                arrived(table.at[f, pl.ds(8 * a, 8)], info_send.at[a, i], info_recv.at[a, i], at.across)

    for tick in range(GROUPS + 3):
        for k in range(4):
            if 0 <= tick - k < GROUPS:
                steps[tick - k][k]()
        if tick == 1:
            spread_info()
    gather_info()
    for copy in sent:
        copy.wait_send()


def dispatch(px, pc, info):
    vmem = pl.BlockSpec(memory_space=pltpu.VMEM)
    return pl.pallas_call(
        dispatch_kernel,
        out_shape=(
            jax.ShapeDtypeStruct((WIDTH, SLOTS), jnp.bfloat16),
            jax.ShapeDtypeStruct((WIDTH, SLOTS), jnp.bfloat16),
            jax.ShapeDtypeStruct((N_HID, N_BLK, 2, 256), jnp.float32),
        ),
        in_specs=[vmem] * 3,
        out_specs=[vmem] * 3,
        scratch_shapes=[
            pltpu.SemaphoreType.DMA((N_BLK, 3)),
            pltpu.SemaphoreType.DMA((N_BLK, 3)),
            pltpu.SemaphoreType.DMA((GROUPS, 14)),
            pltpu.SemaphoreType.DMA((GROUPS, 14)),
            pltpu.SemaphoreType.DMA((2, N_HID)),
            pltpu.SemaphoreType.DMA((2, N_HID)),
            pltpu.SemaphoreType.DMA((3,)),
        ],
        compiler_params=pltpu.CompilerParams(
            collective_id=0, has_side_effects=True, vmem_limit_bytes=56 * 2**20
        ),
    )(px, pc, info)


def combine_kernel(
    part, gate_part, back, gate_back,
    first_a, second_a, third_a, first_b, second_b, mine_b, total, gate_in, gate_sum,
    ring_send, ring_recv, back_send, back_recv, gate_send, gate_recv, local_sem,
):
    at = Place()
    owners = [(at.earlier(j), at.home(j // 8)) for j in range(N_BLK)]
    greet(owners[1:] + [at.hid_peer(i) for i in range(1, N_HID)])
    sent = []
    wide = jnp.float32

    def put(ref, value):
        ref[...] = value.astype(ref.dtype)

    def ring(g):
        a = g // (GROUPS // 2)
        zf = at.home(a) % 2
        lanes_a = pl.ds(g * LANES, HALF)
        start_b = g * LANES + HALF
        lanes_b = pl.ds(start_b, HALF)

        def mine(x, z, lanes):
            return part.at[rows_of(x * 2 + z), lanes]

        def go(src, dst, k, device):
            send(src, dst, ring_send.at[g, k], ring_recv.at[g, k], device, sent)

        def come(region, k):
            arrived(region, ring_send.at[g, k], ring_recv.at[g, k], at.across)

        def first():
            for x in range(4):
                go(mine(x, 1 - zf, lanes_b), first_b.at[g, x], 8 + x, at.across)
            go(mine(at.x_far, 0, lanes_a), first_a.at[g, 0], 0, at.right)
            go(mine(at.x_far, 1, lanes_a), first_a.at[g, 1], 1, at.left)
            go(mine(at.x_right, 1, lanes_a), second_a.at[g, 1], 2, at.right)
            go(mine(at.x_left, 0, lanes_a), second_a.at[g, 2], 3, at.left)

        def second():
            come(first_a.at[g, 0], 0)
            put(
                third_a.at[g, 0],
                first_a[g, 0].astype(wide) + mine(at.x_right, 0, lanes_a)[...].astype(wide),
            )
            go(third_a.at[g, 0], second_a.at[g, 0], 4, at.right)
            come(first_a.at[g, 1], 1)
            put(
                third_a.at[g, 1],
                first_a[g, 1].astype(wide) + mine(at.x_left, 1, lanes_a)[...].astype(wide),
            )
            go(third_a.at[g, 1], second_a.at[g, 3], 5, at.left)
            for x in range(4):
                come(first_b.at[g, x], 8 + x)
            for i, x in enumerate((at.x_far, at.x_right, at.x_left, at.x)):
                put(
                    mine_b.at[g, i],
                    first_b[g, x].astype(wide) + mine(x, zf, lanes_b)[...].astype(wide),
                )
                if i == 0:
                    go(mine_b.at[g, 0, :, pl.ds(0, HALF // 2)], second_b.at[g, 0], 12, at.right)
                    go(mine_b.at[g, 0, :, pl.ds(HALF // 2, HALF // 2)], second_b.at[g, 1], 13, at.left)
                if i == 1:
                    go(mine_b.at[g, 1, :, pl.ds(HALF // 2, HALF // 2)], second_b.at[g, 2], 14, at.right)
                if i == 2:
                    go(mine_b.at[g, 2, :, pl.ds(0, HALF // 2)], second_b.at[g, 3], 15, at.left)

        def third():
            come(second_a.at[g, 0], 4)
            come(second_a.at[g, 1], 2)
            come(second_a.at[g, 2], 3)
            come(second_a.at[g, 3], 5)
            sums = [
                second_a[g, z].astype(wide)
                + second_a[g, 2 + z].astype(wide)
                + mine(at.x, z, lanes_a)[...].astype(wide)
                for z in range(2)
            ]
            keep = jnp.where(zf == 0, sums[0], sums[1])
            give = jnp.where(zf == 0, sums[1], sums[0])
            put(third_a.at[g, 2], give)
            go(third_a.at[g, 2], third_a.at[g, 3], 6, at.across)
            put(total.at[g, :, pl.ds(0, HALF)], keep)
            come(second_b.at[g, 0], 12)
            put(
                second_b.at[g, 4],
                second_b[g, 0].astype(wide) + mine_b[g, 1, :, pl.ds(0, HALF // 2)].astype(wide),
            )
            go(second_b.at[g, 4], second_b.at[g, 6], 16, at.right)
            come(second_b.at[g, 1], 13)
            put(
                second_b.at[g, 5],
                second_b[g, 1].astype(wide) + mine_b[g, 2, :, pl.ds(HALF // 2, HALF // 2)].astype(wide),
            )
            go(second_b.at[g, 5], second_b.at[g, 7], 17, at.left)

        def fourth():
            come(third_a.at[g, 3], 6)
            put(
                total.at[g, :, pl.ds(0, HALF)],
                total[g, :, pl.ds(0, HALF)].astype(wide) + third_a[g, 3].astype(wide),
            )
            come(second_b.at[g, 6], 16)
            come(second_b.at[g, 2], 14)
            come(second_b.at[g, 3], 15)
            come(second_b.at[g, 7], 17)
            for i, (l, r) in enumerate(((6, 3), (2, 7))):
                put(
                    total.at[g, :, pl.ds(HALF + i * (HALF // 2), HALF // 2)],
                    second_b[g, l].astype(wide)
                    + second_b[g, r].astype(wide)
                    + mine_b[g, 3, :, pl.ds(i * (HALF // 2), HALF // 2)].astype(wide),
                )
            for i in range(LANES // CAP):
                j = g * (LANES // CAP) + i
                src = total.at[g, :, pl.ds(i * CAP, CAP)]
                dst = back.at[:, block_of(at.blk)]
                if j == 0:
                    pltpu.make_async_copy(src, dst, local_sem.at[0]).start()
                else:
                    send(src, dst, back_send.at[j, 0], back_recv.at[j, 0], owners[j], sent)

        return first, second, third, fourth

    steps = [ring(g) for g in range(GROUPS)]

    def gate_first():
        for a in range(2):
            cols = pl.ds(8 * a, 8)
            for i in range(1, N_HID):
                q = (at.hid + i) % 8
                f = q if a == 0 else q + 1 - 2 * (q % 2)
                send(
                    gate_part.at[f, cols], gate_in.at[i, cols], gate_send.at[a, i], gate_recv.at[a, i],
                    at.hid_peer(i), sent,
                )

    def gate_second():
        for a in range(2):
            cols = pl.ds(8 * a, 8)
            value = gate_part[at.home(a), cols]
            for i in range(1, N_HID):
                arrived(gate_in.at[i, cols], gate_send.at[a, i], gate_recv.at[a, i], at.across)
                value = value + gate_in[i, cols]
            gate_sum[cols] = value
        for j in range(N_BLK):
            src, dst = gate_sum.at[j], gate_back.at[at.blk]
            if j == 0:
                pltpu.make_async_copy(src, dst, local_sem.at[1]).start()
            else:
                send(src, dst, back_send.at[j, 1], back_recv.at[j, 1], owners[j], sent)

    for tick in range(GROUPS + 3):
        for k in range(4):
            if 0 <= tick - k < GROUPS:
                steps[tick - k][k]()
        if tick == 0:
            gate_first()
        if tick == 2:
            gate_second()
    for j in range(N_BLK):
        e = at.later(j)
        if j == 0:
            pltpu.make_async_copy(total.at[0, :, pl.ds(0, CAP)], back.at[:, block_of(e)], local_sem.at[0]).wait()
            pltpu.make_async_copy(gate_sum.at[0], gate_back.at[e], local_sem.at[1]).wait()
        else:
            arrived(back.at[:, block_of(e)], back_send.at[j, 0], back_recv.at[j, 0], at.across)
            arrived(gate_back.at[e], back_send.at[j, 1], back_recv.at[j, 1], at.across)
    for copy in sent:
        copy.wait_send()


def combine(part, gate_part):
    vmem = pl.BlockSpec(memory_space=pltpu.VMEM)
    bf16, f32 = jnp.bfloat16, jnp.float32
    return pl.pallas_call(
        combine_kernel,
        out_shape=(
            jax.ShapeDtypeStruct((NARROW, SLOTS), bf16),
            jax.ShapeDtypeStruct((N_BLK, 2, 256), f32),
        ),
        in_specs=[vmem] * 2,
        out_specs=[vmem] * 2,
        scratch_shapes=[
            pltpu.VMEM((GROUPS, 2, NARROW, HALF), bf16),
            pltpu.VMEM((GROUPS, 4, NARROW, HALF), bf16),
            pltpu.VMEM((GROUPS, 4, NARROW, HALF), bf16),
            pltpu.VMEM((GROUPS, 4, NARROW, HALF), bf16),
            pltpu.VMEM((GROUPS, 8, NARROW, HALF // 2), bf16),
            pltpu.VMEM((GROUPS, 4, NARROW, HALF), bf16),
            pltpu.VMEM((GROUPS, NARROW, LANES), bf16),
            pltpu.VMEM((N_HID, N_BLK, 2, 256), f32),
            pltpu.VMEM((N_BLK, 2, 256), f32),
            pltpu.SemaphoreType.DMA((GROUPS, 18)),
            pltpu.SemaphoreType.DMA((GROUPS, 18)),
            pltpu.SemaphoreType.DMA((N_BLK, 2)),
            pltpu.SemaphoreType.DMA((N_BLK, 2)),
            pltpu.SemaphoreType.DMA((2, N_HID)),
            pltpu.SemaphoreType.DMA((2, N_HID)),
            pltpu.SemaphoreType.DMA((2,)),
        ],
        compiler_params=pltpu.CompilerParams(
            collective_id=1, has_side_effects=True, vmem_limit_bytes=56 * 2**20
        ),
    )(part, gate_part)


def finish_kernel(sums, grads, sums_all, grads_all, send_sem, recv_sem, local_sem):
    at = Place()
    hid_peers = [at.hid_peer(i) for i in range(1, N_HID)]
    blk_peers = [((at.blk + i) % N_BLK, at.hid) for i in range(1, N_BLK)]
    greet(hid_peers + blk_peers)
    sent = []
    keep = [
        pltpu.make_async_copy(sums, sums_all.at[at.hid], local_sem.at[0]),
        pltpu.make_async_copy(grads, grads_all.at[at.blk], local_sem.at[1]),
    ]
    for i, peer in enumerate(hid_peers):
        send(sums, sums_all.at[at.hid], send_sem.at[i], recv_sem.at[i], peer, sent)
    for i, peer in enumerate(blk_peers):
        send(grads, grads_all.at[at.blk], send_sem.at[8 + i], recv_sem.at[8 + i], peer, sent)
    for copy in keep:
        copy.start()
    for i in range(7):
        arrived(sums_all.at[(at.hid + 7 - i) % 8], send_sem.at[i], recv_sem.at[i], at.across)
    for i in range(15):
        arrived(grads_all.at[(at.blk + 15 - i) % 16], send_sem.at[8 + i], recv_sem.at[8 + i], at.across)
    for copy in keep:
        copy.wait()
    for copy in sent:
        copy.wait_send()


def finish(sums, grads):
    vmem = pl.BlockSpec(memory_space=pltpu.VMEM)
    return pl.pallas_call(
        finish_kernel,
        out_shape=(
            jax.ShapeDtypeStruct((N_HID, *sums.shape), jnp.float32),
            jax.ShapeDtypeStruct((N_BLK, *grads.shape), jnp.float32),
        ),
        in_specs=[vmem] * 2,
        out_specs=[vmem] * 2,
        scratch_shapes=[
            pltpu.SemaphoreType.DMA((23,)),
            pltpu.SemaphoreType.DMA((23,)),
            pltpu.SemaphoreType.DMA((2,)),
        ],
        compiler_params=pltpu.CompilerParams(collective_id=2, has_side_effects=True),
    )(sums, grads)


def gelu_both(values):
    square = values * values
    inner = gelu_factor * (values + gelu_cubic * values * square)
    tangent = jnp.tanh(inner)
    slope = 0.5 * (1.0 + tangent) + 0.5 * values * (1.0 - tangent * tangent) * gelu_factor * (
        1.0 + 3.0 * gelu_cubic * square
    )
    return 0.5 * values * (1.0 + tangent), slope


def on_device(
    tokens,
    cotangent,
    route_weight,
    expert_ids,
    timesteps,
    time_table,
    up_weight,
    down_weight,
    modulation_weight,
    modulation_bias,
):
    tok_count, width = tokens.shape
    f32, bf16 = jnp.float32, jnp.bfloat16
    column_first = lax.axis_index("hid") * NARROW
    image_count = timesteps.shape[0]
    per_image = tok_count // image_count

    condition = jax.nn.silu(
        jnp.concatenate(
            [lax.dynamic_slice_in_dim(time_table, timesteps[b], 1, 0) for b in range(image_count)], axis=0
        )
    )
    mod_part = (
        jnp.einsum("bi,icd->bcd", condition, modulation_weight, precision=lax.Precision.HIGHEST)
        + modulation_bias[None]
    )
    own_tok = jnp.repeat(mod_part, per_image, axis=0)
    inputs = tokens.astype(f32)
    row_mean = jnp.mean(inputs, axis=1, keepdims=True)
    spread = jnp.mean((inputs - row_mean) ** 2, axis=1, keepdims=True)
    inv_spread = 1.0 / jnp.sqrt(spread + norm_epsilon)
    own_inputs = lax.dynamic_slice_in_dim(tokens, column_first, NARROW, 1).astype(f32)
    normed_own = (own_inputs - row_mean) * inv_spread
    hin_own = (normed_own * (1.0 + own_tok[:, 1]) + own_tok[:, 0]).astype(bf16)

    experts = jnp.arange(N_BLK, dtype=jnp.int32)
    named = [(expert_ids[:, k, None] == experts[None, :]) for k in range(2)]
    both = (named[0] | named[1]).astype(bf16)
    earlier = jnp.tril(jnp.ones((tok_count, tok_count), bf16), -1)
    before = jnp.dot(earlier, both, preferred_element_type=f32)
    slot = [jnp.sum(jnp.where(n, before, 0.0), axis=1).astype(jnp.int32) for n in named]
    target = [expert_ids[:, k] * CAP + slot[k] for k in range(2)]
    slot_ids = jnp.arange(SLOTS, dtype=jnp.int32)
    hits = [(t[:, None] == slot_ids[None, :]) for t in target]
    chosen = (hits[0] | hits[1]).astype(bf16)
    weight_of_slot = jnp.sum(
        jnp.where(hits[0], route_weight[:, 0, None], 0.0) + jnp.where(hits[1], route_weight[:, 1, None], 0.0),
        axis=0,
    )

    def to_slots(values):
        return lax.dot_general(values, chosen, (((0,), (0,)), ((), ())), preferred_element_type=f32)

    px = to_slots(hin_own).astype(bf16)
    pc = (to_slots(cotangent) * weight_of_slot[None, :]).astype(bf16)
    first_count = before[per_image]
    condition_parts = condition.reshape(image_count, N_BLK, width // N_BLK).transpose(1, 0, 2)
    info = jnp.concatenate(
        [
            jnp.broadcast_to(mod_part[None, :, 2], (N_BLK, image_count, NARROW)),
            jnp.broadcast_to(first_count[:, None, None], (N_BLK, image_count, 16)),
            condition_parts,
            jnp.zeros((N_BLK, image_count, 256 - NARROW - 16 - width // N_BLK), f32),
        ],
        axis=2,
    )
    rows_in, rows_wc, table = dispatch(px, pc, info)

    up_matrix = up_weight[0]
    down_matrix = down_weight[0]
    own_table = table[lax.axis_index("hid"), :8], table[
        lax.axis_index("hid") + 1 - 2 * (lax.axis_index("hid") % 2), 8:
    ]
    own_table = jnp.concatenate(own_table, axis=0)
    first_of = own_table[:, 0, NARROW]
    is_first = jnp.arange(CAP, dtype=f32)[None, :] < first_of[:, None]
    gates = table[..., :NARROW].transpose(0, 3, 1, 2).reshape(width, N_BLK, 2)
    wc = rows_wc.reshape(width, N_BLK, CAP).astype(f32)
    gated = jnp.where(is_first[None], gates[:, :, 0, None], gates[:, :, 1, None])
    rows_cot = (gated * wc).astype(bf16).reshape(width, SLOTS)
    pre_act = lax.dot_general(up_matrix, rows_in, (((0,), (0,)), ((), ())), preferred_element_type=f32)
    act, slope = gelu_both(pre_act)
    act = act.astype(bf16)
    act_grad = jnp.dot(down_matrix, rows_cot, preferred_element_type=f32)
    pre_grad = (act_grad * slope).astype(bf16)
    up_grads = lax.dot_general(rows_in, pre_grad, (((1,), (1,)), ((), ())), preferred_element_type=f32)[None]
    down_grads = lax.dot_general(act, rows_cot, (((1,), (1,)), ((), ())), preferred_element_type=f32)[None]
    out_rows = lax.dot_general(down_matrix, act, (((0,), (0,)), ((), ())), preferred_element_type=f32)
    grad_rows = jnp.dot(up_matrix, pre_grad, preferred_element_type=f32).astype(bf16)
    product = out_rows.reshape(width, N_BLK, CAP) * wc
    of_first = jnp.sum(jnp.where(is_first[None], product, 0.0), axis=2)
    of_second = jnp.sum(jnp.where(is_first[None], 0.0, product), axis=2)
    gate_part = jnp.stack([of_first, of_second], axis=2).reshape(N_HID, NARROW, N_BLK, 2).transpose(0, 2, 3, 1)
    gate_part = jnp.pad(gate_part, ((0, 0), (0, 0), (0, 0), (0, 256 - NARROW)))
    back, gate_back = combine(grad_rows, gate_part)

    mixed_grad = lax.dot_general(chosen, back, (((1,), (1,)), ((), ())), preferred_element_type=f32)
    shift_grad = jnp.sum(mixed_grad.reshape(image_count, per_image, NARROW), axis=1)
    scale_grad = jnp.sum((mixed_grad * normed_own).reshape(image_count, per_image, NARROW), axis=1)
    gate_grad = jnp.sum(gate_back, axis=0)[:, :NARROW]
    modulation_grads = jnp.concatenate([shift_grad, scale_grad, gate_grad], axis=0)
    norm_grad = mixed_grad * (1.0 + own_tok[:, 1])
    sums = jnp.stack([jnp.sum(norm_grad, axis=1), jnp.sum(norm_grad * normed_own, axis=1)])
    sums_all, grads_all = finish(
        jnp.pad(sums, ((0, 6), (0, 0))), jnp.pad(modulation_grads, ((0, 2), (0, 256 - NARROW)))
    )
    means = jnp.sum(sums_all[:, :2], axis=0) / width
    token_grads = (
        cotangent.astype(f32) + inv_spread * (norm_grad - means[0][:, None] - normed_own * means[1][:, None])
    ).astype(bf16)
    image_grads = grads_all[:, :6, :NARROW].reshape(N_BLK, 3, image_count, NARROW)
    at_blk = lax.axis_index("blk")
    order = jnp.array([shift(j) for j in range(N_BLK)], jnp.int32)
    sources = (at_blk // 8 + order[:, 0]) % 2 * 8 + (at_blk % 8 + 8 - order[:, 1]) % 8
    conditions = own_table[:, :, NARROW + 16 : NARROW + 16 + width // N_BLK]
    modulation_weight_grads = jnp.einsum(
        "jbi,jcbd->icd", conditions, image_grads[sources], precision=lax.Precision.HIGHEST
    )
    modulation_bias_grads = jnp.sum(image_grads, axis=(0, 2))
    return (token_grads, up_grads, down_grads, modulation_weight_grads, modulation_bias_grads)


def solution(mesh):
    in_specs = (
        P("blk", None),
        P("blk", "hid"),
        P("blk", None),
        P("blk", None),
        P("blk"),
        P(),
        P("blk", None, "hid"),
        P("blk", "hid", None),
        P(None, None, "hid"),
        P(None, "hid"),
    )
    out_specs = (
        P("blk", "hid"),
        P("blk", None, "hid"),
        P("blk", "hid", None),
        P("blk", None, "hid"),
        P(None, "hid"),
    )
    return jax.shard_map(
        on_device, mesh=mesh, in_specs=in_specs, out_specs=out_specs, check_vma=False
    )
```

time: 844 us -> 265 us (0.31)
  waiting for transfers between devices: 490 us -> 0 us
  Pallas kernels: 0 us -> 151 us
  blocking collectives: 100 us -> 0 us
  local copies, waits for them, and re-layouts: 102 us -> 21.9 us
  starting transfers between devices: 23.6 us -> 0 us
  other arithmetic: 51.8 us -> 31.2 us
  between operations: 15.2 us -> 5.33 us
    unnamed x5 -> x0, waiting for transfers between devices: 376 us -> none
    pallas_call x0 -> x3, Pallas kernels: none -> 151 us  [the longest x1 85.4 us: dispatch(): pl.pallas_call(dispatch_kernel, out_shape=(jax.ShapeDtypeStruct((WIDTH, S...]
    all_to_all x3 -> x0, waiting for transfers between devices: 114 us -> none  [the longest x1 48.9 us: on_device(): lax.all_to_all(send_cot.reshape(blk_count, capacity, width), 'blk', split...]
    psum x2 -> x0, blocking collectives: 52.9 us -> none  [the longest x1 37 us: on_device(): modulation_bias_grads = lax.psum(jnp.sum(modulation_grads, axis=0), 'blk')]
    all_gather x1 -> x0, blocking collectives: 47.3 us -> none  [on_device(): mod_full = lax.all_gather(mod_part, 'hid', axis=2, tiled=True)]
    gather x4 -> x1, local copies, waits for them, and re-layouts: 35.7 us -> 0.78 us  [on_device(): image_grads[sources]]
    another operation x5 -> x2, local copies, waits for them, and re-layouts: 25.4 us -> 0.63 us  [on_device(): jnp.stack([of_first, of_second], axis=2).reshape(N_HID, NARROW, N_BLK, 2)]
    all_to_all x3 -> x0, starting transfers between devices: 23.1 us -> none  [the longest x1 9.35 us: on_device(): lax.all_to_all(send_in.reshape(blk_count, capacity, width), 'blk', split_...]
  transfers between devices with their start and end apart: 6 -> 0, of which waited for: 4 -> 0; matrix products, arithmetic and copies ran while one was open for 10% -> 0% of each run, Pallas kernels for 0% -> 0%
where the time goes in v1:
time: 265 us; the launch traced here: 262 us
  Pallas kernels  151 us (57%)
  matrix products  52.9 us (20%)
  other arithmetic  31.2 us (12%)
  local copies, waits for them, and re-layouts  21.9 us (8%)
  between operations  5.33 us (2%)
    pallas_call x1, Pallas kernels, dispatch(): pl.pallas_call(dispatch_kernel, out_shape=(jax.ShapeDtypeStruct((WIDTH, S...  85.4 us
    pallas_call x1, Pallas kernels, combine(): pl.pallas_call(combine_kernel, out_shape=(jax.ShapeDtypeStruct((NARROW, S...  55.2 us
    convert_element_type x1, other arithmetic, on_device(): rows_cot = (gated * wc).astype(bf16).reshape(width, SLOTS)  10.9 us
    pallas_call x1, Pallas kernels, finish(): pl.pallas_call(finish_kernel, out_shape=(jax.ShapeDtypeStruct((N_HID, *su...  10.1 us
    dot_general x1, matrix products, on_device(): lax.dot_general(act, rows_cot, (((1,), (1,)), ((), ())), preferred_elemen...  8.83 us
    dot_general x1, matrix products, on_device(): lax.dot_general(up_matrix, rows_in, (((0,), (0,)), ((), ())), preferred_e...  8.2 us
    dot_general x1, matrix products, on_device(): act_grad = jnp.dot(down_matrix, rows_cot, preferred_element_type=f32)  7.39 us
    dot_general x1, matrix products, on_device(): jnp.dot(up_matrix, pre_grad, preferred_element_type=f32).astype(bf16)  7.13 us

profile of v1, /device:TPU:1, one launch (start us, length us, event | category | flops | bytes accessed | tf_op | source)
XLA Modules:
  0.0 262.1 jit_solution(6179698457037626382)
XLA Ops:
  0.7 0.8 fusion.62
  1.6 1.3 fusion.75
  6.8 1.5 convert_reduce_fusion
  8.3 1.7 fusion.15
  12.2 0.8 fusion.70
  13.1 2.6 convolution_add_fusion
  16.4 1.8 add_reduce_fusion
  19.1 1.1 constant_dynamic-slice_fusion.4
  20.4 2.1 fusion.16.pc
  23.8 2.2 convolution_convert_fusion.1.px
  26.0 85.4 %shard_map.146 = (bf16[1152,2048]{1,0:T(8,128)(2,1)}, bf16[1152,2048]{1,0:T(8,128)(2,1)}, f32[8,16,2,256]{3,2,1,0:T(2,128)}) custom-call(bf16[144,2048]{1,0:T(8,128)(2,1)} %convolution_convert_fusion.1.px, bf16[144,2048]{1,0:T(8,128)(2,1)} %fusion.16.pc, f32[16,2,256]{2,1,0:T(2,128)} %maximum_maximum_fusion.info), custom_call_target="tpu_custom_call" | custom-call | tf_op jit(solution)/shard_map/pallas_call | solution.py:202
  112.1 1.0 slice_bitcast_fusion.1
  114.5 8.2 %fusion.26 = f32[2048,576]{0,1:T(8,128)} fusion(bf16[1152,2048]{1,0:T(8,128)(2,1)} %get-tuple-element.14, bf16[1,1152,576]{1,2,0:T(8,128)(2,1)} %param.17), kind=kOutput, calls=%fused_computation.43 | convolution fusion | flops 2717908992 | bytes 10764288 | tf_op jit(solution)/shard_map/dot_general | solution.py:568
  122.7 2.6 %broadcast_in_dim.146 = f32[1152,16,128]{2,1,0:T(8,128)S(1)} broadcast(f32[1152,16]{1,0:T(8,128)S(1)} %copy.78), dimensions={0,1} | broadcast | bytes 9510912 | tf_op jit(solution)/shard_map/jit(_where)/broadcast_in_dim | solution.py:566
  125.4 2.6 %broadcast_in_dim.143 = f32[1152,16,128]{2,1,0:T(8,128)S(1)} broadcast(f32[1152,16]{1,0:T(8,128)S(1)} %copy.77), dimensions={0,1} | broadcast | bytes 9510912 | tf_op jit(solution)/shard_map/jit(_where)/broadcast_in_dim | solution.py:566
  128.1 10.9 %fusion = bf16[1152,2048]{1,0:T(8,128)(2,1)S(1)} fusion(bf16[1152,2048]{1,0:T(8,128)(2,1)S(1)} %bitcast.157, f32[144,8,16,128]{3,2,1,0:T(8,128)S(1)} %bitcast.153, f32[144,8,16,128]{3,2,1,0:T(8,128)S(1)} %bitcast.154, pred[2048]{0:T(1024)(128)(4,1)S(1)} %bitcast_compare_fusion), kind=kLoop, calls=%fused_computation.3 | loop fusion | flops 9437184 | bytes 28313600 | tf_op jit(solution)/shard_map/convert_element_type | solution.py:567
  139.0 7.4 %fusion.6 = bf16[576,2048]{1,0:T(8,128)(2,1)S(1)} fusion(f32[2048,576]{0,1:T(8,128)} %fusion.26, bf16[1152,2048]{1,0:T(8,128)(2,1)S(1)} %fusion, bf16[1,576,1152]{2,1,0:T(8,128)(2,1)S(1)} %copy-done.11), kind=kOutput, calls=%fused_computation.18 | convolution fusion | flops 2739142656 | bytes 13123584 | tf_op jit(solution)/shard_map/dot_general | solution.py:571
  146.4 8.8 %convolution_bitcast_fusion = f32[1,576,1152]{2,1,0:T(8,128)} fusion(bf16[1152,2048]{1,0:T(8,128)(2,1)S(1)} %fusion, f32[2048,576]{0,1:T(8,128)} %fusion.26), kind=kOutput, calls=%fused_computation.25 | convolution fusion | flops 2728525824 | bytes 12091392 | tf_op jit(solution)/shard_map/dot_general | solution.py:574
  155.3 4.8 %convolution_bitcast_fusion.1 = f32[1,1152,576]{1,2,0:T(8,128)} fusion(bf16[1152,2048]{1,0:T(8,128)(2,1)S(1)} %bitcast.182, bf16[576,2048]{1,0:T(8,128)(2,1)S(1)} %fusion.6), kind=kOutput, calls=%fused_computation.26 | convolution fusion | flops 2717908992 | bytes 9732096 | tf_op jit(solution)/shard_map/dot_general | solution.py:573
  160.0 4.3 %fusion.1 = f32[144,8,16,128]{3,1,2,0:T(8,128)S(1)} fusion(bf16[1152,2048]{1,0:T(8,128)(2,1)S(1)} %bitcast.157, bf16[1,576,1152]{2,1,0:T(8,128)(2,1)S(1)} %copy-done.12, f32[2048,576]{0,1:T(8,128)S(1)} %bitcast.184), kind=kOutput, calls=%fused_computation.4 | convolution fusion | flops 2733244416 | bytes 20201472 | tf_op jit(solution)/shard_map/dot_general | solution.py:575
  164.4 2.5 copy.100
  166.9 5.4 %select_reduce_fusion.1 = (f32[1152,16]{1,0:T(8,128)S(1)}, f32[1152,16]{1,0:T(8,128)S(1)}) fusion(f32[1152,16,128]{2,1,0:T(8,128)S(1)} %bitcast.155, pred[16,128]{1,0:T(8,128)(4,1)S(1)} %iota_compare_fusion.8), kind=kLoop, calls=%fused_computation.7 | loop fusion | flops 9400320 | bytes 9586688 | tf_op jit(solution)/shard_map/reduce_sum | solution.py:578
  174.0 7.1 %fusion.2.part = bf16[1152,2048]{1,0:T(8,128)(2,1)} fusion(bf16[576,2048]{1,0:T(8,128)(2,1)} %copy-done.14, bf16[1,1152,576]{1,2,0:T(8,128)(2,1)S(1)} %copy-done.13), kind=kOutput, calls=%fused_computation.9 | convolution fusion | flops 2720268288 | bytes 8404992 | tf_op jit(solution)/shard_map/dot_general | solution.py:576
  181.1 55.2 %shard_map.147 = (bf16[144,2048]{1,0:T(8,128)(2,1)}, f32[16,2,256]{2,1,0:T(2,128)}) custom-call(bf16[1152,2048]{1,0:T(8,128)(2,1)} %fusion.2.part, f32[8,16,2,256]{3,2,1,0:T(2,128)} %pad.12.gate_part), custom_call_target="tpu_custom_call" | custom-call | tf_op jit(solution)/shard_map/pallas_call | solution.py:400
  236.4 3.2 %fusion.69 = (f32[512]{0:T(512)S(1)}, f32[512]{0:T(512)S(1)}, f32[512,144]{0,1:T(8,128)}, f32[512,144]{0,1:T(8,128)S(1)}) fusion(f32[512,3,144]{0,2,1:T(8,128)S(1)} %copy-done.3, f32[512]{0:T(512)S(1)} %add_rsqrt_fusion, f32[512]{0:T(512)S(1)} %broadcast_multiply_fusion.1, bf16[512,144]{0,1:T(8,128)(2,1)S(1)} %copy.97, ...), kind=kOutput, calls=%fused_computation.138 | convolution fusion | flops 305798144 | bytes 1634304 | tf_op jit(solution)/shard_map/dot_general | solution.py:584
  240.8 1.1 reshape.111
  243.4 1.3 select_maximum_fusion.1.grads
  244.7 10.1 %shard_map.148 = (f32[8,8,512]{2,1,0:T(8,128)}, f32[16,8,256]{2,1,0:T(8,128)}) custom-call(f32[8,512]{1,0:T(8,128)} %select_maximum_fusion.sums, f32[8,256]{1,0:T(8,128)} %select_maximum_fusion.1.grads), custom_call_target="tpu_custom_call" | custom-call | tf_op jit(solution)/shard_map/pallas_call | solution.py:460
  254.9 0.9 slice_reduce_fusion
  255.8 1.8 add_convert_fusion
  257.6 0.9 slice_reduce_fusion.2
  260.0 1.8 convolution_bitcast_fusion.2
  (98 shorter events, 13.3 us)
Async XLA Ops:
  0.6 12.5 %copy-start = (f32[1152,3,144]{0,2,1:T(8,128)S(1)}, f32[1152,3,144]{0,2,1:T(8,128)}, u32[]{:S(2)}) copy-start(f32[1152,3,144]{0,2,1:T(8,128)} %param.19) | copy-start | bytes 5971972
  0.6 15.7 %copy-start.9 = (s32[512,2]{0,1:T(2,128)S(1)}, s32[512,2]{0,1:T(2,128)}, u32[]{:S(2)}) copy-start(s32[512,2]{0,1:T(2,128)} %param.14) | copy-start | bytes 12292
  0.7 19.8 %copy-start.6 = (bf16[512,144]{0,1:T(8,128)(2,1)S(1)}, bf16[512,144]{0,1:T(8,128)(2,1)}, u32[]{:S(2)}) copy-start(bf16[512,144]{0,1:T(8,128)(2,1)} %param.12) | copy-start | bytes 442372
  8.3 228.0 %copy-start.8 = (f32[512]{0:T(512)}, f32[512]{0:T(512)S(1)}, u32[]{:S(2)}) copy-start(f32[512]{0:T(512)S(1)} %broadcast_multiply_fusion.1) | copy-start | bytes 6148
  10.1 226.3 %copy-start.10 = (f32[512]{0:T(512)}, f32[512]{0:T(512)S(1)}, u32[]{:S(2)}) copy-start(f32[512]{0:T(512)S(1)} %add_rsqrt_fusion) | copy-start | bytes 6148
  20.4 215.9 %copy-start.4 = (bf16[512,144]{0,1:T(8,128)(2,1)}, bf16[512,144]{0,1:T(8,128)(2,1)S(1)}, u32[]{:S(2)}) copy-start(bf16[512,144]{0,1:T(8,128)(2,1)S(1)} %copy.97) | copy-start | bytes 442372
  23.8 90.3 %copy-start.2 = (f32[512,3,144]{0,2,1:T(8,128)}, f32[512,3,144]{0,2,1:T(8,128)S(1)}, u32[]{:S(2)}) copy-start(f32[512,3,144]{0,2,1:T(8,128)S(1)} %reshape.108) | copy-start | bytes 2654212
  113.4 0.6 copy-start.5
  122.7 5.3 %slice-start = ((s8[4718592]{0:T(1024)(128)(4,1)}), s8[4194304]{0:T(1024)(128)(4,1)S(1)}, s32[]{:S(2)}) async-start(s8[4718592]{0:T(1024)(128)(4,1)} %bitcast.156), calls=%async_computation | async-start | bytes 8388608
  125.4 2.7 %slice-start.1 = ((s8[4718592]{0:T(1024)(128)(4,1)}), s8[524288]{0:T(1024)(128)(4,1)S(1)}, s32[]{:S(2)}) async-start(s8[4718592]{0:T(1024)(128)(4,1)} %bitcast.156), calls=%async_computation.1 | async-start | bytes 1048576
  128.1 10.9 %copy-start.11 = (bf16[1,576,1152]{2,1,0:T(8,128)(2,1)S(1)}, bf16[1,576,1152]{2,1,0:T(8,128)(2,1)}, u32[]{:S(2)}) copy-start(bf16[1,576,1152]{2,1,0:T(8,128)(2,1)} %param.18) | copy-start | bytes 3981316
  128.1 27.2 %slice-start.2 = ((s8[4718592]{0:T(1024)(128)(4,1)}), s8[4194304]{0:T(1024)(128)(4,1)S(1)}, s32[]{:S(2)}) async-start(s8[4718592]{0:T(1024)(128)(4,1)} %bitcast.181), calls=%async_computation.2 | async-start | bytes 8388608
  139.0 16.3 %slice-start.3 = ((s8[4718592]{0:T(1024)(128)(4,1)}), s8[524288]{0:T(1024)(128)(4,1)S(1)}, s32[]{:S(2)}) async-start(s8[4718592]{0:T(1024)(128)(4,1)} %bitcast.181), calls=%async_computation.3 | async-start | bytes 1048576
  139.0 21.1 %slice-start.4 = ((s8[4718592]{0:T(1024)(128)(4,1)}), s8[4194304]{0:T(1024)(128)(4,1)S(1)}, s32[]{:S(2)}) async-start(s8[4718592]{0:T(1024)(128)(4,1)} %bitcast.183), calls=%async_computation.4 | async-start | bytes 8388608
  146.4 8.8 %copy-start.14 = (bf16[576,2048]{1,0:T(8,128)(2,1)}, bf16[576,2048]{1,0:T(8,128)(2,1)S(1)}, u32[]{:S(2)}) copy-start(bf16[576,2048]{1,0:T(8,128)(2,1)S(1)} %fusion.6) | copy-start | bytes 7077892
  146.4 13.6 %slice-start.5 = ((s8[4718592]{0:T(1024)(128)(4,1)}), s8[524288]{0:T(1024)(128)(4,1)S(1)}, s32[]{:S(2)}) async-start(s8[4718592]{0:T(1024)(128)(4,1)} %bitcast.183), calls=%async_computation.5 | async-start | bytes 1048576
  155.2 4.8 %copy-start.12 = (bf16[1,576,1152]{2,1,0:T(8,128)(2,1)S(1)}, bf16[1,576,1152]{2,1,0:T(8,128)(2,1)}, u32[]{:S(2)}) copy-start(bf16[1,576,1152]{2,1,0:T(8,128)(2,1)} %param.18) | copy-start | bytes 3981316
  166.9 7.1 %copy-start.13 = (bf16[1,1152,576]{1,2,0:T(8,128)(2,1)S(1)}, bf16[1,1152,576]{1,2,0:T(8,128)(2,1)}, u32[]{:S(2)}) copy-start(bf16[1,1152,576]{1,2,0:T(8,128)(2,1)} %param.17) | copy-start | bytes 3981316
  181.1 55.3 %copy-start.3 = (f32[512,3,144]{0,2,1:T(8,128)S(1)}, f32[512,3,144]{0,2,1:T(8,128)}, u32[]{:S(2)}) copy-start(f32[512,3,144]{0,2,1:T(8,128)} %copy-done.2) | copy-start | bytes 2654212
  236.3 3.3 %copy-start.7 = (f32[16,2,256]{2,1,0:T(2,128)S(1)}, f32[16,2,256]{2,1,0:T(2,128)}, u32[]{:S(2)}) copy-start(f32[16,2,256]{2,1,0:T(2,128)} %get-tuple-element.16) | copy-start | bytes 98308
  236.3 25.6 %copy-start.1 = (f32[1152,3,144]{0,2,1:T(8,128)S(1)}, f32[1152,3,144]{0,2,1:T(8,128)}, u32[]{:S(2)}) copy-start(f32[1152,3,144]{0,2,1:T(8,128)} %param.19) | copy-start | bytes 5971972

commit v2 on v1

--- a/solution.py
+++ b/solution.py
@@ -80,30 +80,54 @@
     return pl.ds(pl.multiple_of(index * CAP, CAP), CAP)
 
 
-def dispatch_kernel(
-    px, pc, info, xt, ct, table, a2a_send, a2a_recv, ring_send, ring_recv, info_send, info_recv, local_sem
+def gelu_both(values):
+    square = values * values
+    inner = gelu_factor * (values + gelu_cubic * values * square)
+    tangent = jnp.tanh(inner)
+    slope = 0.5 * (1.0 + tangent) + 0.5 * values * (1.0 - tangent * tangent) * gelu_factor * (
+        1.0 + 3.0 * gelu_cubic * square
+    )
+    return 0.5 * values * (1.0 + tangent), slope
+
+
+def dot(a, b, contract=(1, 0), precision=None):
+    return lax.dot_general(
+        a, b, (((contract[0],), (contract[1],)), ((), ())), precision=precision, preferred_element_type=jnp.float32
+    )
+
+
+def expert_kernel(
+    px, pc, info, up, down,
+    back, gate_back, own_info, up_grads, down_grads,
+    xt, ct, hcot, act, pre_grad, part, up_t, down_t, table, gate_rows, gate_part,
+    first_a, second_a, third_a, first_b, second_b, mine_b, total, gate_in, gate_sum, gate_out,
+    a2a_send, a2a_recv, ring_send, ring_recv, info_send, info_recv,
+    sum_send, sum_recv, back_send, back_recv, gate_send, gate_recv, local_sem,
 ):
     at = Place()
+    wide = jnp.float32
     peers = [(at.later(j), at.home(j // 8)) for j in range(N_BLK)]
+    owners = [(at.earlier(j), at.home(j // 8)) for j in range(N_BLK)]
     greet(peers[1:] + [at.hid_peer(i) for i in range(1, N_HID)])
     own = rows_of(at.hid)
     sent = []
     local = []
-    for j in range(N_BLK):
-        lanes = pl.ds(j * CAP, CAP)
-        target = at.later(j)
-        parts = (
-            (px.at[:, block_of(target)], xt.at[own, lanes]),
-            (pc.at[:, block_of(target)], ct.at[own, lanes]),
-            (info.at[target], table.at[at.hid, j]),
-        )
-        for i, (src, dst) in enumerate(parts):
+    for i in (2, 0, 1):
+        for j in range(N_BLK):
+            lanes = pl.ds(j * CAP, CAP)
+            target = at.later(j)
+            src, dst = (
+                (px.at[:, block_of(target)], xt.at[own, lanes]),
+                (pc.at[:, block_of(target)], ct.at[own, lanes]),
+                (info.at[target], table.at[at.hid, j]),
+            )[i]
             if j == 0:
                 copy = pltpu.make_async_copy(src, dst, local_sem.at[i])
                 copy.start()
-                local.append(copy)
+                local.append((i, copy))
             else:
                 send(src, dst, a2a_send.at[j, i], a2a_recv.at[j, i], peers[j], sent)
+    local = dict(local)
 
     def from_peer(j, i, region):
         if j == 0:
@@ -111,7 +135,10 @@
         else:
             arrived(region, a2a_send.at[j, i], a2a_recv.at[j, i], peers[j])
 
-    def ring(g):
+    def put(ref, value):
+        ref[...] = value.astype(ref.dtype)
+
+    def spread(g):
         a = g // (GROUPS // 2)
         f = at.home(a)
         other = at.home(1 - a)
@@ -168,8 +195,6 @@
 
         return first, second, third, fourth
 
-    steps = [ring(g) for g in range(GROUPS)]
-
     def spread_info():
         for a in range(2):
             f = at.home(a)
@@ -185,73 +210,96 @@
                 q = (at.hid + 8 - i) % 8
                 f = q if a == 0 else q + 1 - 2 * (q % 2)
                 arrived(table.at[f, pl.ds(8 * a, 8)], info_send.at[a, i], info_recv.at[a, i], at.across)
-
-    for tick in range(GROUPS + 3):
-        for k in range(4):
-            if 0 <= tick - k < GROUPS:
-                steps[tick - k][k]()
-        if tick == 1:
-            spread_info()
-    gather_info()
-    for copy in sent:
-        copy.wait_send()
-
-
-def dispatch(px, pc, info):
-    vmem = pl.BlockSpec(memory_space=pltpu.VMEM)
-    return pl.pallas_call(
-        dispatch_kernel,
-        out_shape=(
-            jax.ShapeDtypeStruct((WIDTH, SLOTS), jnp.bfloat16),
-            jax.ShapeDtypeStruct((WIDTH, SLOTS), jnp.bfloat16),
-            jax.ShapeDtypeStruct((N_HID, N_BLK, 2, 256), jnp.float32),
-        ),
-        in_specs=[vmem] * 3,
-        out_specs=[vmem] * 3,
-        scratch_shapes=[
-            pltpu.SemaphoreType.DMA((N_BLK, 3)),
-            pltpu.SemaphoreType.DMA((N_BLK, 3)),
-            pltpu.SemaphoreType.DMA((GROUPS, 14)),
-            pltpu.SemaphoreType.DMA((GROUPS, 14)),
-            pltpu.SemaphoreType.DMA((2, N_HID)),
-            pltpu.SemaphoreType.DMA((2, N_HID)),
-            pltpu.SemaphoreType.DMA((3,)),
-        ],
-        compiler_params=pltpu.CompilerParams(
-            collective_id=0, has_side_effects=True, vmem_limit_bytes=56 * 2**20
-        ),
-    )(px, pc, info)
-
-
-def combine_kernel(
-    part, gate_part, back, gate_back,
-    first_a, second_a, third_a, first_b, second_b, mine_b, total, gate_in, gate_sum,
-    ring_send, ring_recv, back_send, back_recv, gate_send, gate_recv, local_sem,
-):
-    at = Place()
-    owners = [(at.earlier(j), at.home(j // 8)) for j in range(N_BLK)]
-    greet(owners[1:] + [at.hid_peer(i) for i in range(1, N_HID)])
-    sent = []
-    wide = jnp.float32
-
-    def put(ref, value):
-        ref[...] = value.astype(ref.dtype)
-
-    def ring(g):
+        for j in range(N_BLK):
+            own_info[j] = table[at.home(j // 8), j]
+            for f in range(N_HID):
+                gate_rows[f, pl.ds(2 * j, 2)] = table[f, j]
+
+    def image_of_lane(g):
+        shape = (2 * N_BLK, LANES)
+        row = lax.broadcasted_iota(jnp.int32, shape, 0)
+        lane = lax.broadcasted_iota(jnp.int32, shape, 1)
+        counts = gate_rows[0, :, pl.ds(128, 128)][:, 16:17].astype(jnp.int32)
+        block = lane // CAP + g * (LANES // CAP)
+        is_first = (lane % CAP) < counts
+        return jnp.where((row // 2 == block) & (is_first == (row % 2 == 0)), 1.0, 0.0).astype(wide)
+
+    def forward(g):
+        lanes = pl.ds(g * LANES, LANES)
+        images = image_of_lane(g)
+
+        @pl.loop(0, N_HID)
+        def _(f):
+            gates = dot(gate_rows[f], images, (0, 0), lax.Precision.HIGHEST)[:NARROW]
+            rows = rows_of(f)
+            hcot[rows, lanes] = (gates * ct[rows, lanes].astype(wide)).astype(hcot.dtype)
+
+        @pl.loop(0, 3)
+        def _(i):
+            rows = pl.ds(pl.multiple_of(i * 192, 64), 192)
+            activated, slope = gelu_both(dot(up_t[rows, :], xt[:, lanes]))
+            act[rows, :] = activated.astype(act.dtype)
+            pre_grad[rows, :] = (dot(down[rows, :], hcot[:, lanes]) * slope).astype(pre_grad.dtype)
+
+        @pl.loop(0, 4)
+        def _(i):
+            rows = rows_of(2 * i, 2)
+            part[rows, lanes] = dot(up[rows, :], pre_grad[...]).astype(part.dtype)
+
+    def gates_of(g):
+        lanes = pl.ds(g * LANES, LANES)
+        images = image_of_lane(g).astype(jnp.bfloat16)
+
+        @pl.loop(0, 4)
+        def _(i):
+            rows = rows_of(2 * i, 2)
+            product = (dot(down_t[rows, :], act[...]) * ct[rows, lanes].astype(wide)).astype(jnp.bfloat16)
+            for k in range(2):
+                value = dot(images, product[k * NARROW : (k + 1) * NARROW], (1, 1))
+                index = 2 * i + k
+                if g == 0:
+                    gate_part[index, :, pl.ds(0, NARROW)] = value
+                else:
+                    gate_part[index, :, pl.ds(0, NARROW)] += value
+
+    def up_weights(g):
+        lanes = pl.ds(g * LANES, LANES)
+
+        @pl.loop(0, 4)
+        def _(i):
+            rows = rows_of(2 * i, 2)
+            value = dot(xt[rows, lanes], pre_grad[...], (1, 1))
+            if g == 0:
+                up_grads[rows, :] = value
+            else:
+                up_grads[rows, :] += value
+
+    def down_weights(g):
+        lanes = pl.ds(g * LANES, LANES)
+
+        @pl.loop(0, 3)
+        def _(i):
+            rows = pl.ds(pl.multiple_of(i * 192, 64), 192)
+            value = dot(act[rows, :], hcot[:, lanes], (1, 1))
+            if g == 0:
+                down_grads[rows, :] = value
+            else:
+                down_grads[rows, :] += value
+
+    def reduce(g):
         a = g // (GROUPS // 2)
         zf = at.home(a) % 2
         lanes_a = pl.ds(g * LANES, HALF)
-        start_b = g * LANES + HALF
-        lanes_b = pl.ds(start_b, HALF)
+        lanes_b = pl.ds(g * LANES + HALF, HALF)
 
         def mine(x, z, lanes):
             return part.at[rows_of(x * 2 + z), lanes]
 
         def go(src, dst, k, device):
-            send(src, dst, ring_send.at[g, k], ring_recv.at[g, k], device, sent)
+            send(src, dst, sum_send.at[g, k], sum_recv.at[g, k], device, sent)
 
         def come(region, k):
-            arrived(region, ring_send.at[g, k], ring_recv.at[g, k], at.across)
+            arrived(region, sum_send.at[g, k], sum_recv.at[g, k], at.across)
 
         def first():
             for x in range(4):
@@ -340,53 +388,77 @@
                 src = total.at[g, :, pl.ds(i * CAP, CAP)]
                 dst = back.at[:, block_of(at.blk)]
                 if j == 0:
-                    pltpu.make_async_copy(src, dst, local_sem.at[0]).start()
+                    pltpu.make_async_copy(src, dst, local_sem.at[3]).start()
                 else:
                     send(src, dst, back_send.at[j, 0], back_recv.at[j, 0], owners[j], sent)
 
         return first, second, third, fourth
 
-    steps = [ring(g) for g in range(GROUPS)]
-
     def gate_first():
         for a in range(2):
-            cols = pl.ds(8 * a, 8)
+            rows = pl.ds(16 * a, 16)
             for i in range(1, N_HID):
                 q = (at.hid + i) % 8
                 f = q if a == 0 else q + 1 - 2 * (q % 2)
                 send(
-                    gate_part.at[f, cols], gate_in.at[i, cols], gate_send.at[a, i], gate_recv.at[a, i],
+                    gate_part.at[f, rows], gate_in.at[i, rows], gate_send.at[a, i], gate_recv.at[a, i],
                     at.hid_peer(i), sent,
                 )
 
     def gate_second():
         for a in range(2):
-            cols = pl.ds(8 * a, 8)
-            value = gate_part[at.home(a), cols]
+            rows = pl.ds(16 * a, 16)
+            value = gate_part[at.home(a), rows]
             for i in range(1, N_HID):
-                arrived(gate_in.at[i, cols], gate_send.at[a, i], gate_recv.at[a, i], at.across)
-                value = value + gate_in[i, cols]
-            gate_sum[cols] = value
+                arrived(gate_in.at[i, rows], gate_send.at[a, i], gate_recv.at[a, i], at.across)
+                value = value + gate_in[i, rows]
+            gate_sum[rows] = value
         for j in range(N_BLK):
-            src, dst = gate_sum.at[j], gate_back.at[at.blk]
+            gate_out[j] = gate_sum[pl.ds(2 * j, 2)]
+            src, dst = gate_out.at[j], gate_back.at[at.blk]
             if j == 0:
-                pltpu.make_async_copy(src, dst, local_sem.at[1]).start()
+                pltpu.make_async_copy(src, dst, local_sem.at[4]).start()
             else:
                 send(src, dst, back_send.at[j, 1], back_recv.at[j, 1], owners[j], sent)
 
-    for tick in range(GROUPS + 3):
+    gate_part[...] = jnp.zeros_like(gate_part)
+
+    @pl.loop(0, 9)
+    def _(i):
+        tile = pl.ds(pl.multiple_of(i * 128, 128), 128)
+        up_t[:, tile] = up[tile, :].T
+        down_t[tile, :] = down[:, tile].T
+
+    spreads = [spread(g) for g in range(GROUPS)]
+    reduces = [reduce(g) for g in range(GROUPS)]
+    for tick in range(GROUPS + 6):
         for k in range(4):
             if 0 <= tick - k < GROUPS:
-                steps[tick - k][k]()
-        if tick == 0:
-            gate_first()
-        if tick == 2:
+                spreads[tick - k][k]()
+            if tick == 0 and k == 0:
+                spread_info()
+        done = tick - 3
+        if done == 0:
+            gather_info()
+        if 0 <= done < GROUPS:
+            forward(done)
+            reduces[done][0]()
+        for k in range(1, 4):
+            if 0 <= done - k < GROUPS:
+                reduces[done - k][k]()
+        if 0 <= done < GROUPS:
+            gates_of(done)
+            if done == GROUPS - 1:
+                gate_first()
+            up_weights(done)
+            down_weights(done)
+        if done == GROUPS:
             gate_second()
     for j in range(N_BLK):
         e = at.later(j)
         if j == 0:
-            pltpu.make_async_copy(total.at[0, :, pl.ds(0, CAP)], back.at[:, block_of(e)], local_sem.at[0]).wait()
-            pltpu.make_async_copy(gate_sum.at[0], gate_back.at[e], local_sem.at[1]).wait()
+            pltpu.make_async_copy(total.at[0, :, pl.ds(0, CAP)], back.at[:, block_of(e)], local_sem.at[3]).wait()
+            pltpu.make_async_copy(gate_out.at[0], gate_back.at[e], local_sem.at[4]).wait()
         else:
             arrived(back.at[:, block_of(e)], back_send.at[j, 0], back_recv.at[j, 0], at.across)
             arrived(gate_back.at[e], back_send.at[j, 1], back_recv.at[j, 1], at.across)
@@ -394,18 +466,34 @@
         copy.wait_send()
 
 
-def combine(part, gate_part):
+def run_experts(px, pc, info, up, down):
     vmem = pl.BlockSpec(memory_space=pltpu.VMEM)
     bf16, f32 = jnp.bfloat16, jnp.float32
+    width, hidden = up.shape
+    dma = pltpu.SemaphoreType.DMA
     return pl.pallas_call(
-        combine_kernel,
+        expert_kernel,
         out_shape=(
             jax.ShapeDtypeStruct((NARROW, SLOTS), bf16),
             jax.ShapeDtypeStruct((N_BLK, 2, 256), f32),
+            jax.ShapeDtypeStruct((N_BLK, 2, 256), f32),
+            jax.ShapeDtypeStruct((width, hidden), f32),
+            jax.ShapeDtypeStruct((hidden, width), f32),
         ),
-        in_specs=[vmem] * 2,
-        out_specs=[vmem] * 2,
+        in_specs=[vmem] * 5,
+        out_specs=[vmem] * 5,
         scratch_shapes=[
+            pltpu.VMEM((width, SLOTS), bf16),
+            pltpu.VMEM((width, SLOTS), bf16),
+            pltpu.VMEM((width, SLOTS), bf16),
+            pltpu.VMEM((hidden, LANES), bf16),
+            pltpu.VMEM((hidden, LANES), bf16),
+            pltpu.VMEM((width, SLOTS), bf16),
+            pltpu.VMEM((hidden, width), bf16),
+            pltpu.VMEM((width, hidden), bf16),
+            pltpu.VMEM((N_HID, N_BLK, 2, 256), f32),
+            pltpu.VMEM((N_HID, 2 * N_BLK, 256), f32),
+            pltpu.VMEM((N_HID, 2 * N_BLK, 256), f32),
             pltpu.VMEM((GROUPS, 2, NARROW, HALF), bf16),
             pltpu.VMEM((GROUPS, 4, NARROW, HALF), bf16),
             pltpu.VMEM((GROUPS, 4, NARROW, HALF), bf16),
@@ -413,20 +501,27 @@
             pltpu.VMEM((GROUPS, 8, NARROW, HALF // 2), bf16),
             pltpu.VMEM((GROUPS, 4, NARROW, HALF), bf16),
             pltpu.VMEM((GROUPS, NARROW, LANES), bf16),
-            pltpu.VMEM((N_HID, N_BLK, 2, 256), f32),
+            pltpu.VMEM((N_HID, 2 * N_BLK, 256), f32),
+            pltpu.VMEM((2 * N_BLK, 256), f32),
             pltpu.VMEM((N_BLK, 2, 256), f32),
-            pltpu.SemaphoreType.DMA((GROUPS, 18)),
-            pltpu.SemaphoreType.DMA((GROUPS, 18)),
-            pltpu.SemaphoreType.DMA((N_BLK, 2)),
-            pltpu.SemaphoreType.DMA((N_BLK, 2)),
-            pltpu.SemaphoreType.DMA((2, N_HID)),
-            pltpu.SemaphoreType.DMA((2, N_HID)),
-            pltpu.SemaphoreType.DMA((2,)),
+            dma((N_BLK, 3)),
+            dma((N_BLK, 3)),
+            dma((GROUPS, 14)),
+            dma((GROUPS, 14)),
+            dma((2, N_HID)),
+            dma((2, N_HID)),
+            dma((GROUPS, 18)),
+            dma((GROUPS, 18)),
+            dma((N_BLK, 2)),
+            dma((N_BLK, 2)),
+            dma((2, N_HID)),
+            dma((2, N_HID)),
+            dma((5,)),
         ],
         compiler_params=pltpu.CompilerParams(
-            collective_id=1, has_side_effects=True, vmem_limit_bytes=56 * 2**20
+            collective_id=0, has_side_effects=True, vmem_limit_bytes=60 * 2**20
         ),
-    )(part, gate_part)
+    )(px, pc, info, up, down)
 
 
 def finish_kernel(sums, grads, sums_all, grads_all, send_sem, recv_sem, local_sem):
@@ -470,18 +565,8 @@
             pltpu.SemaphoreType.DMA((23,)),
             pltpu.SemaphoreType.DMA((2,)),
         ],
-        compiler_params=pltpu.CompilerParams(collective_id=2, has_side_effects=True),
+        compiler_params=pltpu.CompilerParams(collective_id=1, has_side_effects=True),
     )(sums, grads)
-
-
-def gelu_both(values):
-    square = values * values
-    inner = gelu_factor * (values + gelu_cubic * values * square)
-    tangent = jnp.tanh(inner)
-    slope = 0.5 * (1.0 + tangent) + 0.5 * values * (1.0 - tangent * tangent) * gelu_factor * (
-        1.0 + 3.0 * gelu_cubic * square
-    )
-    return 0.5 * values * (1.0 + tangent), slope
 
 
 def on_device(
@@ -551,35 +636,7 @@
         ],
         axis=2,
     )
-    rows_in, rows_wc, table = dispatch(px, pc, info)
-
-    up_matrix = up_weight[0]
-    down_matrix = down_weight[0]
-    own_table = table[lax.axis_index("hid"), :8], table[
-        lax.axis_index("hid") + 1 - 2 * (lax.axis_index("hid") % 2), 8:
-    ]
-    own_table = jnp.concatenate(own_table, axis=0)
-    first_of = own_table[:, 0, NARROW]
-    is_first = jnp.arange(CAP, dtype=f32)[None, :] < first_of[:, None]
-    gates = table[..., :NARROW].transpose(0, 3, 1, 2).reshape(width, N_BLK, 2)
-    wc = rows_wc.reshape(width, N_BLK, CAP).astype(f32)
-    gated = jnp.where(is_first[None], gates[:, :, 0, None], gates[:, :, 1, None])
-    rows_cot = (gated * wc).astype(bf16).reshape(width, SLOTS)
-    pre_act = lax.dot_general(up_matrix, rows_in, (((0,), (0,)), ((), ())), preferred_element_type=f32)
-    act, slope = gelu_both(pre_act)
-    act = act.astype(bf16)
-    act_grad = jnp.dot(down_matrix, rows_cot, preferred_element_type=f32)
-    pre_grad = (act_grad * slope).astype(bf16)
-    up_grads = lax.dot_general(rows_in, pre_grad, (((1,), (1,)), ((), ())), preferred_element_type=f32)[None]
-    down_grads = lax.dot_general(act, rows_cot, (((1,), (1,)), ((), ())), preferred_element_type=f32)[None]
-    out_rows = lax.dot_general(down_matrix, act, (((0,), (0,)), ((), ())), preferred_element_type=f32)
-    grad_rows = jnp.dot(up_matrix, pre_grad, preferred_element_type=f32).astype(bf16)
-    product = out_rows.reshape(width, N_BLK, CAP) * wc
-    of_first = jnp.sum(jnp.where(is_first[None], product, 0.0), axis=2)
-    of_second = jnp.sum(jnp.where(is_first[None], 0.0, product), axis=2)
-    gate_part = jnp.stack([of_first, of_second], axis=2).reshape(N_HID, NARROW, N_BLK, 2).transpose(0, 2, 3, 1)
-    gate_part = jnp.pad(gate_part, ((0, 0), (0, 0), (0, 0), (0, 256 - NARROW)))
-    back, gate_back = combine(grad_rows, gate_part)
+    back, gate_back, own_info, up_grads, down_grads = run_experts(px, pc, info, up_weight[0], down_weight[0])
 
     mixed_grad = lax.dot_general(chosen, back, (((1,), (1,)), ((), ())), preferred_element_type=f32)
     shift_grad = jnp.sum(mixed_grad.reshape(image_count, per_image, NARROW), axis=1)
@@ -599,12 +656,12 @@
     at_blk = lax.axis_index("blk")
     order = jnp.array([shift(j) for j in range(N_BLK)], jnp.int32)
     sources = (at_blk // 8 + order[:, 0]) % 2 * 8 + (at_blk % 8 + 8 - order[:, 1]) % 8
-    conditions = own_table[:, :, NARROW + 16 : NARROW + 16 + width // N_BLK]
+    conditions = own_info[:, :, NARROW + 16 : NARROW + 16 + width // N_BLK]
     modulation_weight_grads = jnp.einsum(
         "jbi,jcbd->icd", conditions, image_grads[sources], precision=lax.Precision.HIGHEST
     )
     modulation_bias_grads = jnp.sum(image_grads, axis=(0, 2))
-    return (token_grads, up_grads, down_grads, modulation_weight_grads, modulation_bias_grads)
+    return (token_grads, up_grads[None], down_grads[None], modulation_weight_grads, modulation_bias_grads)
 
 
 def solution(mesh):

time: 265 us -> 208 us (0.78)
  matrix products: 52.9 us -> 14 us
  other arithmetic: 31.2 us -> 10.3 us
  Pallas kernels: 151 us -> 156 us
    dot_general x6 -> x0, matrix products: 40.6 us -> none  [the longest x1 8.83 us: on_device(): lax.dot_general(act, rows_cot, (((1,), (1,)), ((), ())), preferred_elemen...]
    convert_element_type x1 -> x0, other arithmetic: 10.9 us -> none  [on_device(): rows_cot = (gated * wc).astype(bf16).reshape(width, SLOTS)]
    unnamed x44 -> x22, local copies, waits for them, and re-layouts: 2.94 us -> 10.3 us
    broadcast_in_dim x5 -> x0, local copies, waits for them, and re-layouts: 5.75 us -> none  [on_device(): jnp.where(is_first[None], gates[:, :, 0, None], gates[:, :, 1, None])]
    reduce_sum x1 -> x0, other arithmetic: 5.37 us -> none  [on_device(): of_first = jnp.sum(jnp.where(is_first[None], product, 0.0), axis=2)]
    pallas_call x2 -> x1, Pallas kernels: 141 us -> 144 us  [run_experts(): pl.pallas_call(expert_kernel, out_shape=(jax.ShapeDtypeStruct((NARROW, SL...]
where the time goes in v2:
time: 208 us; the launch traced here: 207 us
  Pallas kernels  156 us (75%)
  local copies, waits for them, and re-layouts  22.1 us (11%)
  matrix products  14 us (7%)
  other arithmetic  10.3 us (5%)
  between operations  4.79 us (2%)
    pallas_call x1, Pallas kernels, run_experts(): pl.pallas_call(expert_kernel, out_shape=(jax.ShapeDtypeStruct((NARROW, SL...  144 us
    pallas_call x1, Pallas kernels, finish(): pl.pallas_call(finish_kernel, out_shape=(jax.ShapeDtypeStruct((N_HID, *su...  12.1 us
    unnamed x22, local copies, waits for them, and re-layouts  10.3 us
    dot_general x2, matrix products, to_slots(): lax.dot_general(values, chosen, (((0,), (0,)), ((), ())), preferred_eleme...  5.43 us

profile of v2, /device:TPU:1, one launch (start us, length us, event | category | flops | bytes accessed | tf_op | source)
XLA Modules:
  0.0 207.3 jit_solution(15955264073476767529)
XLA Ops:
  0.7 1.4 fusion.60
  6.0 0.8 fusion.55
  6.8 2.6 %convolution_add_fusion = f32[2,3,144]{2,0,1:T(2,128)S(1)} fusion(f32[1152,3,144]{0,2,1:T(8,128)S(1)} %copy-done, f32[1,1152]{1,0:T(1,128)S(1)} %get-tuple-element.53, f32[1,1152]{1,0:T(1,128)S(1)} %get-tuple-element.49, f32[3,144]{1,0:T(4,128)} %param.20), kind=kOutput, calls=%fused_computation.21 | convolution fusion | flops 11956320 | bytes 2005056 | tf_op jit(solution)/shard_map/bi,icd->bcd/dot_general | solution.py:596
  9.6 0.8 fusion.59
  10.4 0.4 select_reduce_fusion.1
  11.0 0.7 maximum_maximum_fusion.info
  11.9 1.4 broadcast_in_dim.74
  13.4 2.8 %reshape.63 = f32[512,3,144]{0,2,1:T(8,128)} reshape(f32[2,256,3,144]{1,0,3,2:T(2,128)} %broadcast_in_dim.74) | data formatting | bytes 1769472 | tf_op jit(solution)/shard_map/reshape | solution.py:599
  16.4 0.8 copy.62
  17.1 0.2 convert_reduce_fusion
  17.4 0.5 fusion.7
  17.8 3.3 %convolution_convert_fusion.px = bf16[144,2048]{1,0:T(8,128)(2,1)} fusion(s32[512]{0:T(512)S(1)} %bitcast.82, s32[512]{0:T(512)S(1)} %bitcast.78, f32[512,3,144]{0,2,1:T(8,128)} %reshape.63, bf16[512,144]{0,1:T(8,128)(2,1)} %copy.62, f32[512]{0:T(512)S(1)} %broadcast_multiply_fusion.1, f32[512]{0:T(512)S(1)} %add_rsqrt_fusion), kind=kOutput, calls=%fused_computation.9 | convolution fusion | flops 305946624 | bytes 1335296 | tf_op jit(solution)/shard_map/dot_general | solution.py:624
  21.2 1.7 add_reduce_fusion
  22.8 2.1 %fusion.8.pc = bf16[144,2048]{1,0:T(8,128)(2,1)} fusion(bf16[512,144]{0,1:T(8,128)(2,1)S(1)} %copy-done.5, s32[512]{0:T(512)S(1)} %bitcast.84, s32[512]{0:T(512)S(1)} %bitcast.80, f32[2048]{0:T(1024)S(1)} %add_reduce_fusion), kind=kOutput, calls=%fused_computation.13 | convolution fusion | flops 305725440 | bytes 749568 | tf_op jit(solution)/shard_map/dot_general | solution.py:624
  25.0 2.7 %copy.53 = bf16[1,1152,576]{2,1,0:T(8,128)(2,1)} copy(bf16[1,1152,576]{1,2,0:T(8,128)(2,1)} %param.17) | data formatting | bytes 2654208 | tf_op args[6]
  27.6 144.1 %shard_map.146 = (bf16[144,2048]{1,0:T(8,128)(2,1)}, f32[16,2,256]{2,1,0:T(2,128)}, f32[16,2,256]{2,1,0:T(2,128)}, f32[1152,576]{1,0:T(8,128)}, f32[576,1152]{1,0:T(8,128)}) custom-call(bf16[144,2048]{1,0:T(8,128)(2,1)} %convolution_convert_fusion.px, bf16[144,2048]{1,0:T(8,128)(2,1)} %fusion.8.pc, f32[16,2,256]{2,1,0:T(2,128)} %maximum_maximum_fusion.info, ...), custom_call_target="tpu_custom_call" | custom-call | tf_op jit(solution)/shard_map/pallas_call | solution.py:474
  171.8 3.7 %fusion.54 = (f32[512]{0:T(512)S(1)}, f32[512]{0:T(512)}, f32[512,144]{0,1:T(8,128)}, f32[512,144]{0,1:T(8,128)S(1)}) fusion(f32[512,3,144]{0,2,1:T(8,128)S(1)} %copy-done.2, f32[512]{0:T(512)S(1)} %add_rsqrt_fusion, f32[512]{0:T(512)S(1)} %broadcast_multiply_fusion.1, bf16[512,144]{0,1:T(8,128)(2,1)S(1)} %copy-done.3, ...), kind=kOutput, calls=%fused_computation.98 | convolution fusion | flops 305798144 | bytes 1634304 | tf_op jit(solution)/shard_map/dot_general | solution.py:641
  175.9 1.2 reshape.65
  177.4 0.8 reduce_sum.124
  178.2 0.6 select_maximum_fusion.1.grads
  178.8 1.3 select_maximum_fusion.sums
  180.1 12.1 %shard_map.147 = (f32[8,8,512]{2,1,0:T(8,128)}, f32[16,8,256]{2,1,0:T(8,128)}) custom-call(f32[8,512]{1,0:T(8,128)} %select_maximum_fusion.sums, f32[8,256]{1,0:T(8,128)} %select_maximum_fusion.1.grads), custom_call_target="tpu_custom_call" | custom-call | tf_op jit(solution)/shard_map/pallas_call | solution.py:555
  192.2 0.9 slice_reduce_fusion.2
  193.3 0.7 fusion.48
  194.0 1.3 gather_fusion
  195.3 0.8 slice.71
  196.1 2.0 convolution_bitcast_fusion
  198.1 3.4 %copy.60 = f32[1,1152,576]{1,2,0:T(8,128)} copy(f32[1,1152,576]{2,1,0:T(8,128)} %bitcast.67) | data formatting | bytes 5308416
  201.5 0.9 slice_reduce_fusion
  202.5 0.8 add_convert_fusion
  203.3 0.6 reduce_sum.128
  203.9 3.4 %copy.70 = f32[1,576,1152]{2,1,0:T(8,128)} copy(f32[1,576,1152]{2,1,0:T(8,128)} %bitcast.68) | data formatting | bytes 5308416
  (47 shorter events, 1.9 us)
Async XLA Ops:
  0.6 6.2 %copy-start = (f32[1152,3,144]{0,2,1:T(8,128)S(1)}, f32[1152,3,144]{0,2,1:T(8,128)}, u32[]{:S(2)}) copy-start(f32[1152,3,144]{0,2,1:T(8,128)} %param.19) | copy-start | bytes 5971972
  0.6 15.5 %copy-start.7 = (s32[512,2]{0,1:T(2,128)S(1)}, s32[512,2]{0,1:T(2,128)}, u32[]{:S(2)}) copy-start(s32[512,2]{0,1:T(2,128)} %param.14) | copy-start | bytes 12292
  0.7 15.5 %copy-start.1 = (bf16[512,1152]{1,0:T(8,128)(2,1)S(1)}, bf16[512,1152]{1,0:T(8,128)(2,1)}, u32[]{:S(2)}) copy-start(bf16[512,1152]{1,0:T(8,128)(2,1)} %param.11) | copy-start | bytes 3538948
  16.2 5.0 %copy-start.8 = (f32[512,2]{0,1:T(2,128)S(1)}, f32[512,2]{0,1:T(2,128)}, u32[]{:S(2)}) copy-start(f32[512,2]{0,1:T(2,128)} %param.13) | copy-start | bytes 12292
  17.1 5.7 %copy-start.5 = (bf16[512,144]{0,1:T(8,128)(2,1)S(1)}, bf16[512,144]{0,1:T(8,128)(2,1)}, u32[]{:S(2)}) copy-start(bf16[512,144]{0,1:T(8,128)(2,1)} %param.12) | copy-start | bytes 442372
  25.0 146.8 %copy-start.2 = (f32[512,3,144]{0,2,1:T(8,128)S(1)}, f32[512,3,144]{0,2,1:T(8,128)}, u32[]{:S(2)}) copy-start(f32[512,3,144]{0,2,1:T(8,128)} %reshape.63) | copy-start | bytes 2654212
  25.0 146.8 %copy-start.3 = (bf16[512,144]{0,1:T(8,128)(2,1)S(1)}, bf16[512,144]{0,1:T(8,128)(2,1)}, u32[]{:S(2)}) copy-start(bf16[512,144]{0,1:T(8,128)(2,1)} %copy.62) | copy-start | bytes 442372
  177.3 25.1 %copy-start.4 = (bf16[512,144]{0,1:T(8,128)(2,1)S(1)}, bf16[512,144]{0,1:T(8,128)(2,1)}, u32[]{:S(2)}) copy-start(bf16[512,144]{0,1:T(8,128)(2,1)} %copy.62) | copy-start | bytes 442372
  195.3 7.2 %copy-start.6 = (bf16[512,144]{0,1:T(8,128)(2,1)S(1)}, bf16[512,144]{0,1:T(8,128)(2,1)}, u32[]{:S(2)}) copy-start(bf16[512,144]{0,1:T(8,128)(2,1)} %param.12) | copy-start | bytes 442372

commit v3 on v2

v3 whole, which is shorter than its diff:
```python
import math

import jax
import jax.numpy as jnp
from jax import lax
from jax.experimental import pallas as pl
from jax.experimental.pallas import tpu as pltpu
from jax.sharding import PartitionSpec as P

MESH = pl.DeviceIdType.MESH
norm_epsilon = 1e-06
gelu_cubic = 0.044715
gelu_factor = math.sqrt(2.0 / math.pi)

N_BLK, N_HID = 16, 8
WIDTH, NARROW, CAP = 1152, 144, 128
TOKENS, PATCHES = 512, 256
SLOTS = N_BLK * CAP
GROUPS = 4
LANES = SLOTS // GROUPS
HALF = LANES // 2
ORDER = (0, 1, 6, 2, 7, 3, 5, 4)


def shift(j):
    return j // 8, ORDER[j % 8]


class Place:
    def __init__(self):
        self.blk = lax.axis_index("blk")
        self.hid = lax.axis_index("hid")
        self.z_hi, self.m = self.blk // 8, self.blk % 8
        self.x, self.z_lo = self.hid // 2, self.hid % 2
        self.x_right, self.x_left, self.x_far = [(self.x + i) % 4 for i in (1, 3, 2)]
        self.right = (self.blk, self.x_right * 2 + self.z_lo)
        self.left = (self.blk, self.x_left * 2 + self.z_lo)
        self.across = (self.blk, self.home(1))

    def home(self, a):
        return self.hid if a == 0 else self.hid + 1 - 2 * self.z_lo

    def later(self, j):
        a, m = shift(j)
        return (self.z_hi + a) % 2 * 8 + (self.m + m) % 8

    def earlier(self, j):
        a, m = shift(j)
        return (self.z_hi + a) % 2 * 8 + (self.m + 8 - m) % 8

    def hid_peer(self, i):
        return (self.blk, (self.hid + i) % 8)


def greet(devices):
    barrier = pltpu.get_barrier_semaphore()
    for device in devices:
        pl.semaphore_signal(barrier, inc=1, device_id=device, device_id_type=MESH)
    pl.semaphore_wait(barrier, len(devices))


def send(src, dst, send_sem, recv_sem, device, sent):
    copy = pltpu.make_async_remote_copy(
        src_ref=src, dst_ref=dst, send_sem=send_sem, recv_sem=recv_sem, device_id=device, device_id_type=MESH
    )
    copy.start()
    sent.append(copy)


def arrived(region, send_sem, recv_sem, device):
    pltpu.make_async_remote_copy(
        src_ref=region, dst_ref=region, send_sem=send_sem, recv_sem=recv_sem, device_id=device, device_id_type=MESH
    ).wait_recv()


def rows_of(slice_index, count=1):
    return pl.ds(pl.multiple_of(slice_index * NARROW, 16), count * NARROW)


def block_of(index):
    return pl.ds(pl.multiple_of(index * CAP, CAP), CAP)


def gelu_both(values):
    square = values * values
    inner = gelu_factor * (values + gelu_cubic * values * square)
    tangent = jnp.tanh(inner)
    slope = 0.5 * (1.0 + tangent) + 0.5 * values * (1.0 - tangent * tangent) * gelu_factor * (
        1.0 + 3.0 * gelu_cubic * square
    )
    return 0.5 * values * (1.0 + tangent), slope


def dot(a, b, contract=(1, 0), precision=None):
    return lax.dot_general(
        a, b, (((contract[0],), (contract[1],)), ((), ())), precision=precision, preferred_element_type=jnp.float32
    )


def modulation_kernel(steps, table, weight, bias, ids, columns, info, rows, lookup_sem):
    f32 = jnp.float32
    copies = [
        pltpu.make_async_copy(table.at[pl.ds(steps[b], 1)], rows.at[pl.ds(b, 1)], lookup_sem.at[b]) for b in range(2)
    ]
    for copy in copies:
        copy.start()
    bias_columns = jnp.concatenate([bias[...], jnp.zeros((3, 256 - NARROW), f32)], axis=1)
    bias_columns = jnp.concatenate([bias_columns, jnp.zeros((125, 256), f32)], axis=0).T
    expert = lax.broadcasted_iota(jnp.int32, (N_BLK, 256), 0)
    named = ((expert == ids[0:1, :256]) | (expert == ids[1:2, :256])).astype(jnp.bfloat16)
    counts = dot(jnp.ones((8, 256), jnp.bfloat16), named, (1, 1))
    for copy in copies:
        copy.wait()
    looked = rows[pl.ds(0, 2)]
    condition = looked / (1.0 + jnp.exp(-looked))
    lane = lax.broadcasted_iota(jnp.int32, (NARROW, 128), 1)
    for c in range(3):
        part = weight[c * NARROW : (c + 1) * NARROW]
        sums = [
            jnp.sum(part * condition[b : b + 1], axis=1, keepdims=True) + bias_columns[:NARROW, c : c + 1]
            for b in range(2)
        ]
        columns[c] = jnp.where(lane == 0, sums[0], sums[1])
    gate = columns[2].astype(f32)
    gate = jnp.concatenate([gate, jnp.zeros((256 - NARROW, 128), f32)], axis=0).T[:8]
    high = gate.astype(jnp.bfloat16).astype(f32)
    middle = (gate - high).astype(jnp.bfloat16).astype(f32)
    low = (gate - high) - middle
    parts = jnp.concatenate([high[:2], middle[:2], low[:2], jnp.zeros((2, 256), f32)], axis=0)[:, :NARROW]
    repeated = jnp.concatenate([condition] * 4, axis=0)
    share = WIDTH // N_BLK
    for e in range(N_BLK):
        info[e] = jnp.concatenate(
            [parts, counts, repeated[:, e * share : (e + 1) * share], jnp.zeros((8, 96 - share), f32)], axis=1
        )


def modulation(timesteps, time_table, weight, bias, ids):
    vmem = pl.BlockSpec(memory_space=pltpu.VMEM)
    f32 = jnp.float32
    return pl.pallas_call(
        modulation_kernel,
        out_shape=(
            jax.ShapeDtypeStruct((3, NARROW, 128), f32),
            jax.ShapeDtypeStruct((N_BLK, 8, 256), f32),
        ),
        in_specs=[pl.BlockSpec(memory_space=pltpu.SMEM), pl.BlockSpec(memory_space=pl.ANY), vmem, vmem, vmem],
        out_specs=[vmem] * 2,
        scratch_shapes=[pltpu.VMEM((8, WIDTH), f32), pltpu.SemaphoreType.DMA((2,))],
        compiler_params=pltpu.CompilerParams(vmem_limit_bytes=24 * 2**20),
    )(timesteps, time_table, weight, bias, ids)


def expert_kernel(
    tokens, cotangent, route, ids, columns, info, up_t, down,
    token_grads, up_grads, down_grads, weight_grads, bias_grads,
    chosen, both, targets, stats, normed, payload, back, gate_back, sums, sums_all, grads, grads_all,
    xt, ct, hcot, act, pre_grad, part, up, down_t, table, gate_lanes, counts, gate_part,
    first_a, second_a, third_a, first_b, second_b, mine_b, total, gate_in, gate_sum, gate_out,
    a2a_send, a2a_recv, ring_send, ring_recv, info_send, info_recv,
    sum_send, sum_recv, back_send, back_recv, gate_send, gate_recv, end_send, end_recv, local_sem,
):
    at = Place()
    wide = jnp.float32
    bf16 = jnp.bfloat16
    peers = [(at.later(j), at.home(j // 8)) for j in range(N_BLK)]
    straight = [(at.later(j), at.hid) for j in range(N_BLK)]
    owners = [(at.earlier(j), at.home(j // 8)) for j in range(N_BLK)]
    straight_owners = [(at.earlier(j), at.hid) for j in range(N_BLK)]
    hid_peers = [at.hid_peer(i) for i in range(N_HID)]
    everyone = peers[1:] + straight[8:] + hid_peers[1:]
    barrier = pltpu.get_barrier_semaphore()
    for device in everyone:
        pl.semaphore_signal(barrier, inc=1, device_id=device, device_id_type=MESH)
    own = rows_of(at.hid)
    sent = []

    def put(ref, value):
        ref[...] = value.astype(ref.dtype)

    @pl.loop(0, TOKENS // 128)
    def _(i):
        rows = pl.ds(pl.multiple_of(i * 128, 128), 128)
        values = tokens[rows, :].astype(wide)
        mean = jnp.sum(values, axis=1, keepdims=True) / WIDTH
        spread_of = jnp.sum((values - mean) ** 2, axis=1, keepdims=True) / WIDTH
        inverse = 1.0 / jnp.sqrt(spread_of + norm_epsilon)
        lane = lax.broadcasted_iota(jnp.int32, (128, 128), 1)
        stats[:, rows] = jnp.where(lane == 0, mean, inverse).T[:8]

    row = lax.broadcasted_iota(jnp.int32, (NARROW, WIDTH), 0)
    column = lax.broadcasted_iota(jnp.int32, (NARROW, WIDTH), 1)
    pick = (column == row + at.hid * NARROW).astype(wide).astype(bf16)
    normed[...] = (dot(pick, tokens[...], (1, 1)) - stats[0:1, :]) * stats[1:2, :]
    for b in range(2):
        half = slice(b * PATCHES, (b + 1) * PATCHES)
        hin = normed[:, half] * (1.0 + columns[1, :, b : b + 1]) + columns[0, :, b : b + 1]
        for k in range(2):
            both[:NARROW, k * TOKENS + b * PATCHES : k * TOKENS + (b + 1) * PATCHES] = hin.astype(bf16)
    for k in range(2):
        weighted = cotangent[...].astype(wide) * route[k : k + 1, :]
        both[NARROW:, k * TOKENS : (k + 1) * TOKENS] = weighted.astype(bf16)

    expert = lax.broadcasted_iota(jnp.int32, (N_BLK, TOKENS), 0)
    named = [(expert == ids[k : k + 1, :]) for k in range(2)]
    earlier_row = lax.broadcasted_iota(jnp.int32, (TOKENS, TOKENS), 0)
    earlier_lane = lax.broadcasted_iota(jnp.int32, (TOKENS, TOKENS), 1)
    before = dot(
        (named[0] | named[1]).astype(wide).astype(bf16), (earlier_row < earlier_lane).astype(wide).astype(bf16)
    )
    for k in range(2):
        slot = jnp.sum(jnp.where(named[k], before, 0.0), axis=0, keepdims=True)
        targets[0:1, k * TOKENS : (k + 1) * TOKENS] = ids[k : k + 1, :] * CAP + slot.astype(jnp.int32)

    gate_part[...] = jnp.zeros_like(gate_part)
    pl.semaphore_wait(barrier, len(everyone))

    for j in range(N_BLK):
        target = at.later(j)
        if j == 0:
            info_local = pltpu.make_async_copy(info.at[target], table.at[0], local_sem.at[2])
            info_local.start()
        else:
            send(info.at[target], table.at[j], a2a_send.at[j, 2], a2a_recv.at[j, 2], straight[j], sent)

    def payload_parts(j):
        lanes = pl.ds(j * CAP, CAP)
        return (
            (payload.at[pl.ds(0, NARROW), lanes], xt.at[own, lanes]),
            (payload.at[pl.ds(NARROW, NARROW), lanes], ct.at[own, lanes]),
        )

    def make_payload(pair):
        hits = []
        for j in (2 * pair, 2 * pair + 1):
            slots = lax.broadcasted_iota(jnp.int32, (CAP, 2 * TOKENS), 0) + at.later(j) * CAP
            hit = (slots == targets[0:1, :]).astype(wide)
            chosen[block_of(at.later(j)), :] = (hit[:, :TOKENS] + hit[:, TOKENS:]).astype(bf16)
            hits.append(hit.astype(bf16))
        value = dot(both[...], jnp.concatenate(hits, axis=0), (1, 1))
        payload[:, 2 * pair * CAP : (2 * pair + 2) * CAP] = value.astype(bf16)
        for j in (2 * pair, 2 * pair + 1):
            for i, (src, dst) in enumerate(payload_parts(j)):
                if j == 0:
                    pltpu.make_async_copy(src, dst, local_sem.at[i]).start()
                else:
                    send(src, dst, a2a_send.at[j, i], a2a_recv.at[j, i], peers[j], sent)

    def from_peer(j, i, region):
        if j == 0:
            pltpu.make_async_copy(*payload_parts(0)[i], local_sem.at[i]).wait()
        else:
            arrived(region, a2a_send.at[j, i], a2a_recv.at[j, i], peers[j])

    def spread(g):
        a = g // (GROUPS // 2)
        f = at.home(a)
        other = at.home(1 - a)
        zf = f % 2
        lanes = pl.ds(g * LANES, LANES)
        halves = [pl.ds(g * LANES + i * HALF, HALF) for i in range(2)]
        far_slice = at.x_far * 2 + zf

        def go(array, rows, cols, k, device):
            region = array.at[rows, cols]
            send(region, region, ring_send.at[g, k], ring_recv.at[g, k], device, sent)

        def come(array, rows, cols, k):
            arrived(array.at[rows, cols], ring_send.at[g, k], ring_recv.at[g, k], at.across)

        def first():
            for j in range(g * LANES // CAP, (g + 1) * LANES // CAP):
                from_peer(j, 0, xt.at[rows_of(f), pl.ds(j * CAP, CAP)])
                from_peer(j, 1, ct.at[rows_of(f), pl.ds(j * CAP, CAP)])
            go(xt, rows_of(f), lanes, 0, at.across)
            go(ct, rows_of(f), lanes, 6, at.right)
            go(ct, rows_of(f), lanes, 7, at.left)
            go(ct, rows_of(f), lanes, 5, at.across)

        def second():
            come(xt, rows_of(other), lanes, 0)
            go(xt, rows_of(at.x * 2, 2), lanes, 1, at.right)
            go(xt, rows_of(at.x * 2, 2), lanes, 2, at.left)
            left, right = rows_of(at.x_left * 2 + zf), rows_of(at.x_right * 2 + zf)
            come(ct, left, lanes, 6)
            go(ct, left, halves[0], 8, at.right)
            go(ct, left, lanes, 10, at.across)
            come(ct, right, lanes, 7)
            go(ct, right, halves[1], 9, at.left)
            go(ct, right, lanes, 11, at.across)

        def third():
            come(xt, rows_of(at.x_left * 2, 2), lanes, 1)
            go(xt, rows_of(at.x_left * 2), lanes, 3, at.right)
            come(xt, rows_of(at.x_right * 2, 2), lanes, 2)
            go(xt, rows_of(at.x_right * 2 + 1), lanes, 4, at.left)
            for i in range(2):
                come(ct, rows_of(far_slice), halves[i], 8 + i)
                go(ct, rows_of(far_slice), halves[i], 12 + i, at.across)

        def fourth():
            come(xt, rows_of(at.x_far * 2), lanes, 3)
            come(xt, rows_of(at.x_far * 2 + 1), lanes, 4)
            come(ct, rows_of(other), lanes, 5)
            come(ct, rows_of(at.x_left * 2 + 1 - zf), lanes, 10)
            come(ct, rows_of(at.x_right * 2 + 1 - zf), lanes, 11)
            for i in range(2):
                come(ct, rows_of(at.x_far * 2 + 1 - zf), halves[i], 12 + i)

        return first, second, third, fourth

    def spread_info():
        info_local.wait()
        for j in range(1, N_BLK):
            arrived(table.at[j], a2a_send.at[j, 2], a2a_recv.at[j, 2], straight[j])
        rows = table[...].reshape(8 * N_BLK, 256)
        gate_lanes[own, :] = rows.T[:NARROW].astype(bf16)
        region = gate_lanes.at[own]
        for i in range(1, N_HID):
            send(region, region, info_send.at[i], info_recv.at[i], hid_peers[i], sent)
        lane = lax.broadcasted_iota(jnp.int32, (8 * N_BLK, 128), 1)
        mine = jnp.sum(jnp.where(lane == at.blk + 16, rows[:, 128:], 0.0), axis=1, keepdims=True)
        counts[...] = jnp.broadcast_to(mine, counts.shape)

    def gather_info():
        for i in range(1, N_HID):
            region = gate_lanes.at[rows_of((at.hid + 8 - i) % 8)]
            arrived(region, info_send.at[i], info_recv.at[i], at.across)

    def image_of_lane(g):
        shape = (8 * N_BLK, LANES)
        row = lax.broadcasted_iota(jnp.int32, shape, 0)
        lane = lax.broadcasted_iota(jnp.int32, shape, 1)
        block = lane // CAP + g * (LANES // CAP)
        first_count = jnp.concatenate([counts[...]] * (LANES // 128), axis=1)
        is_first = (lane % CAP).astype(wide) < first_count
        hit = (row // 8 == block) & (is_first == (row % 2 == 0)) & (row % 8 < 6)
        return jnp.where(hit, 1.0, 0.0).astype(bf16)

    def forward(g):
        lanes = pl.ds(g * LANES, LANES)
        images = image_of_lane(g)

        @pl.loop(0, 4)
        def _(i):
            rows = rows_of(2 * i, 2)
            gates = dot(gate_lanes[rows, :], images)
            hcot[rows, lanes] = (gates * ct[rows, lanes].astype(wide)).astype(bf16)

        @pl.loop(0, 3)
        def _(i):
            rows = pl.ds(pl.multiple_of(i * 192, 64), 192)
            activated, slope = gelu_both(dot(up_t[rows, :], xt[:, lanes]))
            act[rows, :] = activated.astype(bf16)
            pre_grad[rows, :] = (dot(down[rows, :], hcot[:, lanes]) * slope).astype(bf16)

        @pl.loop(0, 4)
        def _(i):
            rows = rows_of(2 * i, 2)
            part[rows, lanes] = dot(up[rows, :], pre_grad[...]).astype(bf16)

    def gates_of(g):
        lanes = pl.ds(g * LANES, LANES)
        spots = 2 * N_BLK
        narrow_row = lax.broadcasted_iota(jnp.int32, (spots, 8 * N_BLK), 0)
        wide_row = lax.broadcasted_iota(jnp.int32, (spots, 8 * N_BLK), 1)
        compact = (wide_row == narrow_row // 2 * 8 + narrow_row % 2).astype(wide).astype(bf16)
        images = dot(compact, image_of_lane(g)).astype(bf16)

        @pl.loop(0, 4)
        def _(i):
            rows = rows_of(2 * i, 2)
            product = (dot(down_t[rows, :], act[...]) * ct[rows, lanes].astype(wide)).astype(bf16)
            for k in range(2):
                value = dot(images, product[k * NARROW : (k + 1) * NARROW], (1, 1))
                gate_part[2 * i + k, :, pl.ds(0, NARROW)] += value

    def weights(grads_of, left, right, g):
        lanes = pl.ds(g * LANES, LANES)

        @pl.loop(0, 3)
        def _(i):
            rows = pl.ds(pl.multiple_of(i * 192, 64), 192)
            value = dot(left[rows, :], right[:, lanes], (1, 1))
            if g == 0:
                grads_of[rows, :] = value
            else:
                grads_of[rows, :] += value

    def reduce(g):
        a = g // (GROUPS // 2)
        zf = at.home(a) % 2
        lanes_a = pl.ds(g * LANES, HALF)
        lanes_b = pl.ds(g * LANES + HALF, HALF)

        def mine(x, z, lanes):
            return part.at[rows_of(x * 2 + z), lanes]

        def go(src, dst, k, device):
            send(src, dst, sum_send.at[g, k], sum_recv.at[g, k], device, sent)

        def come(region, k):
            arrived(region, sum_send.at[g, k], sum_recv.at[g, k], at.across)

        def first():
            for x in range(4):
                go(mine(x, 1 - zf, lanes_b), first_b.at[g, x], 8 + x, at.across)
            go(mine(at.x_far, 0, lanes_a), first_a.at[g, 0], 0, at.right)
            go(mine(at.x_far, 1, lanes_a), first_a.at[g, 1], 1, at.left)
            go(mine(at.x_right, 1, lanes_a), second_a.at[g, 1], 2, at.right)
            go(mine(at.x_left, 0, lanes_a), second_a.at[g, 2], 3, at.left)

        def second():
            come(first_a.at[g, 0], 0)
            put(
                third_a.at[g, 0],
                first_a[g, 0].astype(wide) + mine(at.x_right, 0, lanes_a)[...].astype(wide),
            )
            go(third_a.at[g, 0], second_a.at[g, 0], 4, at.right)
            come(first_a.at[g, 1], 1)
            put(
                third_a.at[g, 1],
                first_a[g, 1].astype(wide) + mine(at.x_left, 1, lanes_a)[...].astype(wide),
            )
            go(third_a.at[g, 1], second_a.at[g, 3], 5, at.left)
            for x in range(4):
                come(first_b.at[g, x], 8 + x)
            for i, x in enumerate((at.x_far, at.x_right, at.x_left, at.x)):
                put(
                    mine_b.at[g, i],
                    first_b[g, x].astype(wide) + mine(x, zf, lanes_b)[...].astype(wide),
                )
                if i == 0:
                    go(mine_b.at[g, 0, :, pl.ds(0, HALF // 2)], second_b.at[g, 0], 12, at.right)
                    go(mine_b.at[g, 0, :, pl.ds(HALF // 2, HALF // 2)], second_b.at[g, 1], 13, at.left)
                if i == 1:
                    go(mine_b.at[g, 1, :, pl.ds(HALF // 2, HALF // 2)], second_b.at[g, 2], 14, at.right)
                if i == 2:
                    go(mine_b.at[g, 2, :, pl.ds(0, HALF // 2)], second_b.at[g, 3], 15, at.left)

        def third():
            come(second_a.at[g, 0], 4)
            come(second_a.at[g, 1], 2)
            come(second_a.at[g, 2], 3)
            come(second_a.at[g, 3], 5)
            sums = [
                second_a[g, z].astype(wide)
                + second_a[g, 2 + z].astype(wide)
                + mine(at.x, z, lanes_a)[...].astype(wide)
                for z in range(2)
            ]
            keep = jnp.where(zf == 0, sums[0], sums[1])
            give = jnp.where(zf == 0, sums[1], sums[0])
            put(third_a.at[g, 2], give)
            go(third_a.at[g, 2], third_a.at[g, 3], 6, at.across)
            put(total.at[g, :, pl.ds(0, HALF)], keep)
            come(second_b.at[g, 0], 12)
            put(
                second_b.at[g, 4],
                second_b[g, 0].astype(wide) + mine_b[g, 1, :, pl.ds(0, HALF // 2)].astype(wide),
            )
            go(second_b.at[g, 4], second_b.at[g, 6], 16, at.right)
            come(second_b.at[g, 1], 13)
            put(
                second_b.at[g, 5],
                second_b[g, 1].astype(wide) + mine_b[g, 2, :, pl.ds(HALF // 2, HALF // 2)].astype(wide),
            )
            go(second_b.at[g, 5], second_b.at[g, 7], 17, at.left)

        def fourth():
            come(third_a.at[g, 3], 6)
            put(
                total.at[g, :, pl.ds(0, HALF)],
                total[g, :, pl.ds(0, HALF)].astype(wide) + third_a[g, 3].astype(wide),
            )
            come(second_b.at[g, 6], 16)
            come(second_b.at[g, 2], 14)
            come(second_b.at[g, 3], 15)
            come(second_b.at[g, 7], 17)
            for i, (l, r) in enumerate(((6, 3), (2, 7))):
                put(
                    total.at[g, :, pl.ds(HALF + i * (HALF // 2), HALF // 2)],
                    second_b[g, l].astype(wide)
                    + second_b[g, r].astype(wide)
                    + mine_b[g, 3, :, pl.ds(i * (HALF // 2), HALF // 2)].astype(wide),
                )
            for i in range(LANES // CAP):
                j = g * (LANES // CAP) + i
                src = total.at[g, :, pl.ds(i * CAP, CAP)]
                dst = back.at[:, block_of(at.blk)]
                if j == 0:
                    pltpu.make_async_copy(src, dst, local_sem.at[3]).start()
                else:
                    send(src, dst, back_send.at[j, 0], back_recv.at[j, 0], owners[j], sent)

        return first, second, third, fourth

    def gate_first():
        for i in range(1, N_HID):
            q = (at.hid + i) % 8
            send(gate_part.at[q], gate_in.at[i], gate_send.at[i], gate_recv.at[i], hid_peers[i], sent)

    def gate_second():
        value = gate_part[at.hid]
        for i in range(1, N_HID):
            arrived(gate_in.at[i], gate_send.at[i], gate_recv.at[i], at.across)
            value = value + gate_in[i]
        gate_sum[...] = value
        for j in range(N_BLK):
            gate_out[j] = gate_sum[pl.ds(2 * j, 2)]
            src, dst = gate_out.at[j], gate_back.at[at.blk]
            if j == 0:
                pltpu.make_async_copy(src, dst, local_sem.at[4]).start()
            else:
                send(src, dst, back_send.at[j, 1], back_recv.at[j, 1], straight_owners[j], sent)

    make_payload(0)
    make_payload(1)

    @pl.loop(0, 9)
    def _(i):
        tile = pl.ds(pl.multiple_of(i * 128, 128), 128)
        up[tile, :] = up_t[:, tile].T
        down_t[tile, :] = down[:, tile].T

    spreads = [spread(g) for g in range(GROUPS)]
    reduces = [reduce(g) for g in range(GROUPS)]
    for tick in range(GROUPS + 6):
        for k in range(4):
            if 0 <= tick - k < GROUPS:
                spreads[tick - k][k]()
            if tick == 0 and k == 0:
                for pair in range(2, N_BLK // 2):
                    make_payload(pair)
                spread_info()
        done = tick - 3
        if done == 0:
            gather_info()
        if 0 <= done < GROUPS:
            forward(done)
            reduces[done][0]()
        for k in range(1, 4):
            if 0 <= done - k < GROUPS:
                reduces[done - k][k]()
        if 0 <= done < GROUPS:
            gates_of(done)
            if done == GROUPS - 1:
                gate_first()
            weights(up_grads, pre_grad, xt, done)
            weights(down_grads, act, hcot, done)
        if done == GROUPS:
            gate_second()

    for j in range(N_BLK):
        e = at.later(j)
        if j == 0:
            pltpu.make_async_copy(total.at[0, :, pl.ds(0, CAP)], back.at[:, block_of(e)], local_sem.at[3]).wait()
            pltpu.make_async_copy(gate_out.at[0], gate_back.at[e], local_sem.at[4]).wait()
        else:
            arrived(back.at[:, block_of(e)], back_send.at[j, 0], back_recv.at[j, 0], at.across)
            arrived(gate_back.at[e], back_send.at[j, 1], back_recv.at[j, 1], at.across)

    mixed = dot(back[...], chosen[...])
    scale = jnp.concatenate(
        [jnp.broadcast_to(1.0 + columns[1, :, b : b + 1], (NARROW, PATCHES)) for b in range(2)], axis=1
    )
    norm_grad = mixed * scale
    sums[0:1, :] = jnp.sum(norm_grad, axis=0, keepdims=True)
    sums[1:2, :] = jnp.sum(norm_grad * normed[...], axis=0, keepdims=True)
    for i in range(1, N_HID):
        send(sums, sums_all.at[i], end_send.at[N_BLK + i], end_recv.at[N_BLK + i], hid_peers[i], sent)
    lane = lax.broadcasted_iota(jnp.int32, (NARROW, 128), 1)
    listed = jnp.zeros((NARROW, 128), wide)
    for c, values in enumerate((mixed, mixed * normed[...])):
        for b in range(2):
            value = jnp.sum(values[:, b * PATCHES : (b + 1) * PATCHES], axis=1, keepdims=True)
            listed = jnp.where(lane == 2 * c + b, value, listed)
    listed = jnp.concatenate([listed, jnp.zeros((256 - NARROW, 128), wide)], axis=0).T
    gate_grad = gate_back[0]
    for e in range(1, N_BLK):
        gate_grad = gate_grad + gate_back[e]
    grads[...] = jnp.concatenate([listed[:4], gate_grad, jnp.zeros((2, 256), wide)], axis=0)
    for j in range(1, N_BLK):
        send(grads, grads_all.at[j], end_send.at[j], end_recv.at[j], straight[j], sent)
    grads_all[0] = grads[...]
    first, second = sums[0:1, :], sums[1:2, :]
    for i in range(1, N_HID):
        arrived(sums_all.at[i], end_send.at[N_BLK + i], end_recv.at[N_BLK + i], at.across)
        first = first + sums_all[i, 0:1, :]
        second = second + sums_all[i, 1:2, :]
    token_grads[...] = (
        cotangent[...].astype(wide)
        + stats[1:2, :] * (norm_grad - first / WIDTH - normed[...] * (second / WIDTH))
    ).astype(bf16)
    for j in range(1, N_BLK):
        arrived(grads_all.at[j], end_send.at[j], end_recv.at[j], at.across)
    image_grads = grads_all[...].reshape(8 * N_BLK, 256)
    conditions = table[...].reshape(8 * N_BLK, 256)[:, 128:]
    kind = lax.broadcasted_iota(jnp.int32, (8 * N_BLK, 128), 0) % 8 // 2
    kind_wide = lax.broadcasted_iota(jnp.int32, (8 * N_BLK, 256), 0) % 8 // 2
    for c in range(3):
        value = dot(jnp.where(kind == c, conditions, 0.0), image_grads, (0, 0), lax.Precision.HIGHEST)
        weight_grads[c] = value[32 : 32 + WIDTH // N_BLK, :NARROW]
        bias_grads[c : c + 1, :] = jnp.sum(jnp.where(kind_wide == c, image_grads, 0.0), axis=0, keepdims=True)[
            :, :NARROW
        ]
    for copy in sent:
        copy.wait_send()


def run_experts(*operands):
    vmem = pl.BlockSpec(memory_space=pltpu.VMEM)
    bf16, f32 = jnp.bfloat16, jnp.float32
    hidden, width = operands[-1].shape
    dma = pltpu.SemaphoreType.DMA
    return pl.pallas_call(
        expert_kernel,
        out_shape=(
            jax.ShapeDtypeStruct((NARROW, TOKENS), bf16),
            jax.ShapeDtypeStruct((hidden, width), f32),
            jax.ShapeDtypeStruct((hidden, width), f32),
            jax.ShapeDtypeStruct((3, width // N_BLK, NARROW), f32),
            jax.ShapeDtypeStruct((3, NARROW), f32),
        ),
        in_specs=[vmem] * len(operands),
        out_specs=[vmem] * 5,
        scratch_shapes=[
            pltpu.VMEM((SLOTS, TOKENS), bf16),
            pltpu.VMEM((2 * NARROW, 2 * TOKENS), bf16),
            pltpu.VMEM((8, 2 * TOKENS), jnp.int32),
            pltpu.VMEM((8, TOKENS), f32),
            pltpu.VMEM((NARROW, TOKENS), f32),
            pltpu.VMEM((2 * NARROW, SLOTS), bf16),
            pltpu.VMEM((NARROW, SLOTS), bf16),
            pltpu.VMEM((N_BLK, 2, 256), f32),
            pltpu.VMEM((2, TOKENS), f32),
            pltpu.VMEM((N_HID, 2, TOKENS), f32),
            pltpu.VMEM((8, 256), f32),
            pltpu.VMEM((N_BLK, 8, 256), f32),
            pltpu.VMEM((width, SLOTS), bf16),
            pltpu.VMEM((width, SLOTS), bf16),
            pltpu.VMEM((width, SLOTS), bf16),
            pltpu.VMEM((hidden, LANES), bf16),
            pltpu.VMEM((hidden, LANES), bf16),
            pltpu.VMEM((width, SLOTS), bf16),
            pltpu.VMEM((width, hidden), bf16),
            pltpu.VMEM((width, hidden), bf16),
            pltpu.VMEM((N_BLK, 8, 256), f32),
            pltpu.VMEM((width, 128), bf16),
            pltpu.VMEM((8 * N_BLK, 128), f32),
            pltpu.VMEM((N_HID, 2 * N_BLK, 256), f32),
            pltpu.VMEM((GROUPS, 2, NARROW, HALF), bf16),
            pltpu.VMEM((GROUPS, 4, NARROW, HALF), bf16),
            pltpu.VMEM((GROUPS, 4, NARROW, HALF), bf16),
            pltpu.VMEM((GROUPS, 4, NARROW, HALF), bf16),
            pltpu.VMEM((GROUPS, 8, NARROW, HALF // 2), bf16),
            pltpu.VMEM((GROUPS, 4, NARROW, HALF), bf16),
            pltpu.VMEM((GROUPS, NARROW, LANES), bf16),
            pltpu.VMEM((N_HID, 2 * N_BLK, 256), f32),
            pltpu.VMEM((2 * N_BLK, 256), f32),
            pltpu.VMEM((N_BLK, 2, 256), f32),
            dma((N_BLK, 3)),
            dma((N_BLK, 3)),
            dma((GROUPS, 14)),
            dma((GROUPS, 14)),
            dma((N_HID,)),
            dma((N_HID,)),
            dma((GROUPS, 18)),
            dma((GROUPS, 18)),
            dma((N_BLK, 2)),
            dma((N_BLK, 2)),
            dma((N_HID,)),
            dma((N_HID,)),
            dma((N_BLK + N_HID,)),
            dma((N_BLK + N_HID,)),
            dma((5,)),
        ],
        compiler_params=pltpu.CompilerParams(
            collective_id=0, has_side_effects=True, vmem_limit_bytes=60 * 2**20
        ),
    )(*operands)


def on_device(
    tokens,
    cotangent,
    route_weight,
    expert_ids,
    timesteps,
    time_table,
    up_weight,
    down_weight,
    modulation_weight,
    modulation_bias,
):
    ids = expert_ids.T
    by_feature = modulation_weight.transpose(1, 2, 0).reshape(3 * NARROW, WIDTH)
    columns, info = modulation(timesteps, time_table, by_feature, modulation_bias, ids)
    token_grads, up_grads, down_grads, weight_grads, bias_grads = run_experts(
        tokens, cotangent.T, route_weight.T, ids, columns, info, up_weight[0].T, down_weight[0]
    )
    return (token_grads.T, up_grads.T[None], down_grads[None], weight_grads.transpose(1, 0, 2), bias_grads)


def solution(mesh):
    in_specs = (
        P("blk", None),
        P("blk", "hid"),
        P("blk", None),
        P("blk", None),
        P("blk"),
        P(),
        P("blk", None, "hid"),
        P("blk", "hid", None),
        P(None, None, "hid"),
        P(None, "hid"),
    )
    out_specs = (
        P("blk", "hid"),
        P("blk", None, "hid"),
        P("blk", "hid", None),
        P("blk", None, "hid"),
        P(None, "hid"),
    )
    return jax.shard_map(
        on_device, mesh=mesh, in_specs=in_specs, out_specs=out_specs, check_vma=False
    )
```

time: 208 us -> 160 us (0.77)
  matrix products: 14 us -> 0 us
  Pallas kernels: 156 us -> 144 us
  other arithmetic: 10.3 us -> 0 us
  local copies, waits for them, and re-layouts: 22.1 us -> 15.2 us
  between operations: 4.79 us -> 0.68 us
    dot_general x6 -> x0, matrix products: 14 us -> none  [the longest x2 5.43 us: to_slots(): lax.dot_general(values, chosen, (((0,), (0,)), ((), ())), preferred_eleme...]
    pallas_call x2, Pallas kernels: 156 us -> 144 us  [the longest x1 143 us: run_experts(): pl.pallas_call(expert_kernel, out_shape=(jax.ShapeDtypeStruct((NARROW, TO...]
    reduce_sum x9 -> x0, other arithmetic: 6.06 us -> none  [the longest x1 1.66 us: on_device(): jnp.sum(jnp.where(hits[0], route_weight[:, 0, None], 0.0) + jnp.where(hit...]
    unnamed x22 -> x25, local copies, waits for them, and re-layouts: 10.3 us -> 15.2 us
    reshape x4 -> x0, local copies, waits for them, and re-layouts: 4.21 us -> none  [the longest x1 2.79 us: on_device(): own_tok = jnp.repeat(mod_part, per_image, axis=0)]
    slice x7 -> x0, local copies, waits for them, and re-layouts: 3.16 us -> none  [the longest x1 1.4 us: on_device(): timesteps[b]]
where the time goes in v3:
time: 160 us
  Pallas kernels  144 us (90%)
  local copies, waits for them, and re-layouts  15.2 us (10%)
    pallas_call x1, Pallas kernels, run_experts(): pl.pallas_call(expert_kernel, out_shape=(jax.ShapeDtypeStruct((NARROW, TO...  143 us
    unnamed x25, local copies, waits for them, and re-layouts  15.2 us

profile of v3, /device:TPU:1, one launch (start us, length us, event | category | flops | bytes accessed | tf_op | source)
XLA Modules:
  0.0 160.0 jit_solution(13209447272377946746)
XLA Ops:
  0.6 0.0 copy-start
  0.6 2.3 %copy-done = f32[1000,1152]{1,0:T(8,128)S(1)} copy-done((f32[1000,1152]{1,0:T(8,128)S(1)}, f32[1000,1152]{1,0:T(8,128)}, u32[]{:S(2)}) %copy-start) | copy-done | bytes 4608024
  2.9 0.0 copy-start.1
  2.9 1.6 copy-done.1
  4.5 0.0 copy-start.4
  4.5 0.7 copy-done.4
  5.2 0.0 copy-start.5
  5.2 0.7 copy-done.5
  5.9 0.0 copy-start.6
  5.9 0.7 copy-done.6
  6.5 1.5 shard_map.137
  8.0 0.0 copy-start.2
  8.0 0.7 copy-done.2
  8.7 0.0 copy-start.3
  8.7 0.7 copy-done.3
  9.4 142.7 %shard_map.138 = (bf16[144,512]{1,0:T(8,128)(2,1)}, f32[576,1152]{1,0:T(8,128)}, f32[576,1152]{1,0:T(8,128)}, f32[3,72,144]{2,1,0:T(8,128)}, f32[3,144]{1,0:T(4,128)}) custom-call(bf16[512,1152]{1,0:T(8,128)(2,1)} %tokens.1, bf16[144,512]{1,0:T(8,128)(2,1)} %bitcast.24, f32[2,512]{1,0:T(2,128)} %bitcast.26, s32[2,512]{1,0:T(2,128)} %bitcast.17, ...), custom_call_target="tpu_custom_call" | custom-call | tf_op jit(solution)/shard_map/pallas_call | solution.py:616
  152.0 1.6 copy.20
  153.6 0.0 copy-start.7
  153.6 3.6 %copy.21 = f32[1,1152,576]{1,2,0:T(8,128)} copy(f32[1,1152,576]{1,2,0:T(8,128)} %bitcast.20) | data formatting | bytes 5308416
  157.2 0.0 copy-done.7
  157.2 0.0 copy-start.8
  157.2 0.0 copy-start.9
  157.2 1.5 copy.22
  158.7 0.0 copy-done.8
  158.7 0.7 copy.23
  159.4 0.0 copy-done.9
  159.4 0.6 copy.24
Async XLA Ops:
  0.6 2.3 %copy-start = (f32[1000,1152]{1,0:T(8,128)S(1)}, f32[1000,1152]{1,0:T(8,128)}, u32[]{:S(2)}) copy-start(f32[1000,1152]{1,0:T(8,128)} %table.1) | copy-start | bytes 13824004
  2.9 1.6 copy-start.1
  4.5 0.7 copy-start.4
  5.2 0.7 copy-start.5
  5.9 0.7 copy-start.6
  8.0 0.7 copy-start.2
  8.7 0.7 copy-start.3
  153.6 3.6 %copy-start.7 = (f32[576,1152]{1,0:T(8,128)S(1)}, f32[576,1152]{1,0:T(8,128)}, u32[]{:S(2)}) copy-start(f32[576,1152]{1,0:T(8,128)} %get-tuple-element.16) | copy-start | bytes 7962628
  157.2 1.5 copy-start.8
  157.2 2.2 %copy-start.9 = (f32[3,144]{1,0:T(4,128)S(1)}, f32[3,144]{1,0:T(4,128)}, u32[]{:S(2)}) copy-start(f32[3,144]{1,0:T(4,128)} %get-tuple-element.28) | copy-start | bytes 5188

commit v4 on v3

--- a/solution.py
+++ b/solution.py
@@ -147,15 +147,15 @@
         in_specs=[pl.BlockSpec(memory_space=pltpu.SMEM), pl.BlockSpec(memory_space=pl.ANY), vmem, vmem, vmem],
         out_specs=[vmem] * 2,
         scratch_shapes=[pltpu.VMEM((8, WIDTH), f32), pltpu.SemaphoreType.DMA((2,))],
-        compiler_params=pltpu.CompilerParams(vmem_limit_bytes=24 * 2**20),
+        compiler_params=pltpu.CompilerParams(vmem_limit_bytes=60 * 2**20),
     )(timesteps, time_table, weight, bias, ids)
 
 
 def expert_kernel(
     tokens, cotangent, route, ids, columns, info, up_t, down,
-    token_grads, up_grads, down_grads, weight_grads, bias_grads,
-    chosen, both, targets, stats, normed, payload, back, gate_back, sums, sums_all, grads, grads_all,
-    xt, ct, hcot, act, pre_grad, part, up, down_t, table, gate_lanes, counts, gate_part,
+    norm_grads, normed, stats, totals, grads_all, table, up_out, down_out,
+    chosen, both, targets, payload, back, gate_back, sums, sums_all, grads, up_grads, down_grads,
+    xt, ct, hcot, act, pre_grad, part, up, down_t, gate_lanes, counts, gate_part,
     first_a, second_a, third_a, first_b, second_b, mine_b, total, gate_in, gate_sum, gate_out,
     a2a_send, a2a_recv, ring_send, ring_recv, info_send, info_recv,
     sum_send, sum_recv, back_send, back_recv, gate_send, gate_recv, end_send, end_recv, local_sem,
@@ -523,6 +523,10 @@
         up[tile, :] = up_t[:, tile].T
         down_t[tile, :] = down[:, tile].T
 
+    results = [
+        pltpu.make_async_copy(up_grads, up_out, local_sem.at[5]),
+        pltpu.make_async_copy(down_grads, down_out, local_sem.at[6]),
+    ]
     spreads = [spread(g) for g in range(GROUPS)]
     reduces = [reduce(g) for g in range(GROUPS)]
     for tick in range(GROUPS + 6):
@@ -548,7 +552,10 @@
                 gate_first()
             weights(up_grads, pre_grad, xt, done)
             weights(down_grads, act, hcot, done)
-        if done == GROUPS:
+            if done == GROUPS - 1:
+                for copy in results:
+                    copy.start()
+        if done == GROUPS + 1:
             gate_second()
 
     for j in range(N_BLK):
@@ -588,12 +595,37 @@
         arrived(sums_all.at[i], end_send.at[N_BLK + i], end_recv.at[N_BLK + i], at.across)
         first = first + sums_all[i, 0:1, :]
         second = second + sums_all[i, 1:2, :]
-    token_grads[...] = (
-        cotangent[...].astype(wide)
-        + stats[1:2, :] * (norm_grad - first / WIDTH - normed[...] * (second / WIDTH))
-    ).astype(bf16)
+    norm_grads[...] = norm_grad
+    totals[...] = jnp.concatenate([first, second], axis=0)
     for j in range(1, N_BLK):
         arrived(grads_all.at[j], end_send.at[j], end_recv.at[j], at.across)
+    for copy in results:
+        copy.wait()
+    for copy in sent:
+        copy.wait_send()
+
+
+def result_kernel(
+    cotangent, norm_grads, normed, stats, totals, grads_all, table, up_in, down_in,
+    token_grads, up_grads, down_grads, weight_grads, bias_grads, held, move_sem,
+):
+    f32 = jnp.float32
+    share = up_in.shape[0] // 4
+    loads, stores = [], []
+    for i, (src, dst) in enumerate(((up_in, up_grads), (down_in, down_grads))):
+        for k in range(4):
+            rows = pl.ds(k * share, share)
+            loads.append(pltpu.make_async_copy(src.at[rows], held.at[i, rows], move_sem.at[0, i, k]))
+            stores.append(pltpu.make_async_copy(held.at[i, rows], dst.at[rows], move_sem.at[1, i, k]))
+    for load in loads:
+        load.start()
+    token_grads[...] = (
+        cotangent[...].astype(f32)
+        + stats[1:2, :] * (norm_grads[...] - totals[0:1, :] / WIDTH - normed[...] * (totals[1:2, :] / WIDTH))
+    ).astype(token_grads.dtype)
+    for load, store in zip(loads, stores):
+        load.wait()
+        store.start()
     image_grads = grads_all[...].reshape(8 * N_BLK, 256)
     conditions = table[...].reshape(8 * N_BLK, 256)[:, 128:]
     kind = lax.broadcasted_iota(jnp.int32, (8 * N_BLK, 128), 0) % 8 // 2
@@ -604,8 +636,28 @@
         bias_grads[c : c + 1, :] = jnp.sum(jnp.where(kind_wide == c, image_grads, 0.0), axis=0, keepdims=True)[
             :, :NARROW
         ]
-    for copy in sent:
-        copy.wait_send()
+    for store in stores:
+        store.wait()
+
+
+def results_of(*operands):
+    vmem, anywhere = pl.BlockSpec(memory_space=pltpu.VMEM), pl.BlockSpec(memory_space=pl.ANY)
+    f32 = jnp.float32
+    hidden, width = operands[-1].shape
+    return pl.pallas_call(
+        result_kernel,
+        out_shape=(
+            jax.ShapeDtypeStruct((NARROW, TOKENS), jnp.bfloat16),
+            jax.ShapeDtypeStruct((hidden, width), f32),
+            jax.ShapeDtypeStruct((hidden, width), f32),
+            jax.ShapeDtypeStruct((3, width // N_BLK, NARROW), f32),
+            jax.ShapeDtypeStruct((3, NARROW), f32),
+        ),
+        in_specs=[vmem] * 7 + [anywhere] * 2,
+        out_specs=[vmem, anywhere, anywhere, vmem, vmem],
+        scratch_shapes=[pltpu.VMEM((2, hidden, width), f32), pltpu.SemaphoreType.DMA((2, 2, 4))],
+        compiler_params=pltpu.CompilerParams(vmem_limit_bytes=60 * 2**20),
+    )(*operands)
 
 
 def run_experts(*operands):
@@ -616,27 +668,29 @@
     return pl.pallas_call(
         expert_kernel,
         out_shape=(
-            jax.ShapeDtypeStruct((NARROW, TOKENS), bf16),
+            jax.ShapeDtypeStruct((NARROW, TOKENS), f32),
+            jax.ShapeDtypeStruct((NARROW, TOKENS), f32),
+            jax.ShapeDtypeStruct((8, TOKENS), f32),
+            jax.ShapeDtypeStruct((2, TOKENS), f32),
+            jax.ShapeDtypeStruct((N_BLK, 8, 256), f32),
+            jax.ShapeDtypeStruct((N_BLK, 8, 256), f32),
             jax.ShapeDtypeStruct((hidden, width), f32),
             jax.ShapeDtypeStruct((hidden, width), f32),
-            jax.ShapeDtypeStruct((3, width // N_BLK, NARROW), f32),
-            jax.ShapeDtypeStruct((3, NARROW), f32),
         ),
         in_specs=[vmem] * len(operands),
-        out_specs=[vmem] * 5,
+        out_specs=[vmem] * 6 + [pl.BlockSpec(memory_space=pl.ANY)] * 2,
         scratch_shapes=[
             pltpu.VMEM((SLOTS, TOKENS), bf16),
             pltpu.VMEM((2 * NARROW, 2 * TOKENS), bf16),
             pltpu.VMEM((8, 2 * TOKENS), jnp.int32),
-            pltpu.VMEM((8, TOKENS), f32),
-            pltpu.VMEM((NARROW, TOKENS), f32),
             pltpu.VMEM((2 * NARROW, SLOTS), bf16),
             pltpu.VMEM((NARROW, SLOTS), bf16),
             pltpu.VMEM((N_BLK, 2, 256), f32),
             pltpu.VMEM((2, TOKENS), f32),
             pltpu.VMEM((N_HID, 2, TOKENS), f32),
             pltpu.VMEM((8, 256), f32),
-            pltpu.VMEM((N_BLK, 8, 256), f32),
+            pltpu.VMEM((hidden, width), f32),
+            pltpu.VMEM((hidden, width), f32),
             pltpu.VMEM((width, SLOTS), bf16),
             pltpu.VMEM((width, SLOTS), bf16),
             pltpu.VMEM((width, SLOTS), bf16),
@@ -645,7 +699,6 @@
             pltpu.VMEM((width, SLOTS), bf16),
             pltpu.VMEM((width, hidden), bf16),
             pltpu.VMEM((width, hidden), bf16),
-            pltpu.VMEM((N_BLK, 8, 256), f32),
             pltpu.VMEM((width, 128), bf16),
             pltpu.VMEM((8 * N_BLK, 128), f32),
             pltpu.VMEM((N_HID, 2 * N_BLK, 256), f32),
@@ -673,7 +726,7 @@
             dma((N_HID,)),
             dma((N_BLK + N_HID,)),
             dma((N_BLK + N_HID,)),
-            dma((5,)),
+            dma((7,)),
         ],
         compiler_params=pltpu.CompilerParams(
             collective_id=0, has_side_effects=True, vmem_limit_bytes=60 * 2**20
@@ -696,9 +749,11 @@
     ids = expert_ids.T
     by_feature = modulation_weight.transpose(1, 2, 0).reshape(3 * NARROW, WIDTH)
     columns, info = modulation(timesteps, time_table, by_feature, modulation_bias, ids)
-    token_grads, up_grads, down_grads, weight_grads, bias_grads = run_experts(
-        tokens, cotangent.T, route_weight.T, ids, columns, info, up_weight[0].T, down_weight[0]
-    )
+    turned = cotangent.T
+    partial_results = run_experts(
+        tokens, turned, route_weight.T, ids, columns, info, up_weight[0].T, down_weight[0]
+    )
+    token_grads, up_grads, down_grads, weight_grads, bias_grads = results_of(turned, *partial_results)
     return (token_grads.T, up_grads.T[None], down_grads[None], weight_grads.transpose(1, 0, 2), bias_grads)
 
 

time: 160 us -> 152 us (0.950)
  local copies, waits for them, and re-layouts: 15.2 us -> 0 us
  Pallas kernels: 144 us -> 151 us
    unnamed x25 -> x0, local copies, waits for them, and re-layouts: 15.2 us -> none
    pallas_call x0 -> x1, Pallas kernels: none -> 6.66 us  [results_of(): pl.pallas_call(result_kernel, out_shape=(jax.ShapeDtypeStruct((NARROW, TO...]
    pallas_call x1, Pallas kernels: 1.48 us -> 3.71 us  [modulation(): pl.pallas_call(modulation_kernel, out_shape=(jax.ShapeDtypeStruct((3, NAR...]
    pallas_call x1, Pallas kernels: 143 us -> 140 us  [run_experts(): pl.pallas_call(expert_kernel, out_shape=(jax.ShapeDtypeStruct((NARROW, TO...]
where the time goes in v4:
time: 152 us
  Pallas kernels  151 us (99%)
    pallas_call x1, Pallas kernels, run_experts(): pl.pallas_call(expert_kernel, out_shape=(jax.ShapeDtypeStruct((NARROW, TO...  140 us
    pallas_call x1, Pallas kernels, results_of(): pl.pallas_call(result_kernel, out_shape=(jax.ShapeDtypeStruct((NARROW, TO...  6.66 us
    pallas_call x1, Pallas kernels, modulation(): pl.pallas_call(modulation_kernel, out_shape=(jax.ShapeDtypeStruct((3, NAR...  3.71 us

profile of v4, /device:TPU:1, one launch (start us, length us, event | category | flops | bytes accessed | tf_op | source)
XLA Modules:
  0.0 151.6 jit_solution(8720651908264741276)
XLA Ops:
  0.6 3.7 %shard_map.137 = (f32[3,144,128]{2,1,0:T(8,128)}, f32[16,8,256]{2,1,0:T(8,128)}) custom-call(s32[2]{0:T(128)} %steps.1, f32[1000,1152]{1,0:T(8,128)} %table.1, f32[432,1152]{1,0:T(8,128)} %bitcast.16, f32[3,144]{1,0:T(4,128)} %bias.1, s32[2,512]{1,0:T(2,128)} %bitcast.21), custom_call_target="tpu_custom_call" | custom-call | tf_op jit(solution)/shard_map/pallas_call | solution.py:141
  4.3 140.4 %shard_map.138 = (f32[144,512]{1,0:T(8,128)}, f32[144,512]{1,0:T(8,128)}, f32[8,512]{1,0:T(8,128)}, f32[2,512]{1,0:T(2,128)}, f32[16,8,256]{2,1,0:T(8,128)}, /*i...) custom-call(bf16[512,1152]{1,0:T(8,128)(2,1)} %tokens.1, bf16[144,512]{1,0:T(8,128)(2,1)} %bitcast.19, ...), custom_call_target="tpu_custom_call" | custom-call | tf_op jit(solution)/shard_map/pallas_call | solution.py:668
  144.8 6.7 %shard_map.139 = (bf16[144,512]{1,0:T(8,128)(2,1)}, f32[576,1152]{1,0:T(8,128)}, f32[576,1152]{1,0:T(8,128)}, f32[3,72,144]{2,1,0:T(8,128)}, f32[3,144]{1,0:T(4,128)}) custom-call(bf16[144,512]{1,0:T(8,128)(2,1)} %bitcast.20, f32[144,512]{1,0:T(8,128)} %get-tuple-element.22.norm_grads, f32[144,512]{1,0:T(8,128)} %get-tuple-element.23.normed, ...), custom_call_target="tpu_custom_call" | custom-call | tf_op jit(solution)/shard_map/pallas_call | solution.py:647

commit v5 on v4

--- a/solution.py
+++ b/solution.py
@@ -120,8 +120,10 @@
             jnp.sum(part * condition[b : b + 1], axis=1, keepdims=True) + bias_columns[:NARROW, c : c + 1]
             for b in range(2)
         ]
-        columns[c] = jnp.where(lane == 0, sums[0], sums[1])
-    gate = columns[2].astype(f32)
+        value = jnp.where(lane % 2 == 0, sums[0], sums[1])
+        listed = value if c == 0 else jnp.where(lane // 2 == c, value, listed)
+    columns[...] = listed
+    gate = value
     gate = jnp.concatenate([gate, jnp.zeros((256 - NARROW, 128), f32)], axis=0).T[:8]
     high = gate.astype(jnp.bfloat16).astype(f32)
     middle = (gate - high).astype(jnp.bfloat16).astype(f32)
@@ -141,7 +143,7 @@
     return pl.pallas_call(
         modulation_kernel,
         out_shape=(
-            jax.ShapeDtypeStruct((3, NARROW, 128), f32),
+            jax.ShapeDtypeStruct((NARROW, 128), f32),
             jax.ShapeDtypeStruct((N_BLK, 8, 256), f32),
         ),
         in_specs=[pl.BlockSpec(memory_space=pltpu.SMEM), pl.BlockSpec(memory_space=pl.ANY), vmem, vmem, vmem],
@@ -154,11 +156,11 @@
 def expert_kernel(
     tokens, cotangent, route, ids, columns, info, up_t, down,
     norm_grads, normed, stats, totals, grads_all, table, up_out, down_out,
-    chosen, both, targets, payload, back, gate_back, sums, sums_all, grads, up_grads, down_grads,
+    chosen, both, four, four_normed, four_columns, targets, payload, four_payload, back, gate_back, sums, sums_all, grads, up_grads, down_grads,
     xt, ct, hcot, act, pre_grad, part, up, down_t, gate_lanes, counts, gate_part,
     first_a, second_a, third_a, first_b, second_b, mine_b, total, gate_in, gate_sum, gate_out,
     a2a_send, a2a_recv, ring_send, ring_recv, info_send, info_recv,
-    sum_send, sum_recv, back_send, back_recv, gate_send, gate_recv, end_send, end_recv, local_sem,
+    sum_send, sum_recv, back_send, back_recv, gate_send, gate_recv, end_send, end_recv, near_send, near_recv, local_sem,
 ):
     at = Place()
     wide = jnp.float32
@@ -194,7 +196,7 @@
     normed[...] = (dot(pick, tokens[...], (1, 1)) - stats[0:1, :]) * stats[1:2, :]
     for b in range(2):
         half = slice(b * PATCHES, (b + 1) * PATCHES)
-        hin = normed[:, half] * (1.0 + columns[1, :, b : b + 1]) + columns[0, :, b : b + 1]
+        hin = normed[:, half] * (1.0 + columns[:, 2 + b : 3 + b]) + columns[:, b : b + 1]
         for k in range(2):
             both[:NARROW, k * TOKENS + b * PATCHES : k * TOKENS + (b + 1) * PATCHES] = hin.astype(bf16)
     for k in range(2):
@@ -213,7 +215,19 @@
         targets[0:1, k * TOKENS : (k + 1) * TOKENS] = ids[k : k + 1, :] * CAP + slot.astype(jnp.int32)
 
     gate_part[...] = jnp.zeros_like(gate_part)
+    row = lax.broadcasted_iota(jnp.int32, (4 * NARROW, WIDTH), 0)
+    column = lax.broadcasted_iota(jnp.int32, (4 * NARROW, WIDTH), 1)
+    wanted = row + jnp.where(row < 2 * NARROW, at.x * 2 * NARROW, (at.x_far - 1) * 2 * NARROW)
+    pick = (column == wanted).astype(wide).astype(bf16)
+    four_normed[...] = (dot(pick, tokens[...], (1, 1)) - stats[0:1, :]) * stats[1:2, :]
+    four_columns[at.z_lo] = columns[...]
     pl.semaphore_wait(barrier, len(everyone))
+
+    near = (at.across, (at.blk, at.x_far * 2 + at.z_lo), (at.blk, at.x_far * 2 + 1 - at.z_lo))
+    near_place = (at.z_lo, 2 + at.z_lo, 2 + at.z_lo)
+    near_from = (1 - at.z_lo, 2 + at.z_lo, 3 - at.z_lo)
+    for i in range(3):
+        send(columns, four_columns.at[near_place[i]], near_send.at[i], near_recv.at[i], near[i], sent)
 
     for j in range(N_BLK):
         target = at.later(j)
@@ -230,14 +244,17 @@
             (payload.at[pl.ds(NARROW, NARROW), lanes], ct.at[own, lanes]),
         )
 
-    def make_payload(pair):
+    def hits_of(pair):
         hits = []
         for j in (2 * pair, 2 * pair + 1):
             slots = lax.broadcasted_iota(jnp.int32, (CAP, 2 * TOKENS), 0) + at.later(j) * CAP
             hit = (slots == targets[0:1, :]).astype(wide)
             chosen[block_of(at.later(j)), :] = (hit[:, :TOKENS] + hit[:, TOKENS:]).astype(bf16)
             hits.append(hit.astype(bf16))
-        value = dot(both[...], jnp.concatenate(hits, axis=0), (1, 1))
+        return jnp.concatenate(hits, axis=0)
+
+    def make_payload(pair):
+        value = dot(both[...], hits_of(pair), (1, 1))
         payload[:, 2 * pair * CAP : (2 * pair + 2) * CAP] = value.astype(bf16)
         for j in (2 * pair, 2 * pair + 1):
             for i, (src, dst) in enumerate(payload_parts(j)):
@@ -245,6 +262,39 @@
                     pltpu.make_async_copy(src, dst, local_sem.at[i]).start()
                 else:
                     send(src, dst, a2a_send.at[j, i], a2a_recv.at[j, i], peers[j], sent)
+
+    def make_four():
+        for i in range(3):
+            arrived(four_columns.at[near_from[i]], near_send.at[i], near_recv.at[i], near[i])
+        for q in range(4):
+            rows = slice(q * NARROW, (q + 1) * NARROW)
+            for b in range(2):
+                half = slice(b * PATCHES, (b + 1) * PATCHES)
+                hin = four_normed[rows, half] * (1.0 + four_columns[q, :, 2 + b : 3 + b])
+                hin = (hin + four_columns[q, :, b : b + 1]).astype(bf16)
+                for k in range(2):
+                    four[rows, k * TOKENS + b * PATCHES : k * TOKENS + (b + 1) * PATCHES] = hin
+
+        four[4 * NARROW :, :] = both[NARROW:, :]
+
+    four_rows = (pl.ds(0, 2 * NARROW), pl.ds(2 * NARROW, 2 * NARROW), pl.ds(4 * NARROW, NARROW))
+
+    def four_parts(j):
+        lanes = pl.ds(j * CAP, CAP)
+        targets_of = (xt.at[rows_of(at.x * 2, 2), lanes], xt.at[rows_of(at.x_far * 2, 2), lanes], ct.at[own, lanes])
+        return [
+            (four_payload.at[rows, pl.ds(j * CAP - LANES, CAP)], dst) for rows, dst in zip(four_rows, targets_of)
+        ]
+
+    def make_four_payload(g):
+        for pair in range(g * LANES // CAP // 2, (g + 1) * LANES // CAP // 2):
+            hits = hits_of(pair)
+            start = 2 * pair * CAP - LANES
+            for rows in four_rows:
+                four_payload[rows, start : start + 2 * CAP] = dot(four[rows, :], hits, (1, 1)).astype(bf16)
+            for j in (2 * pair, 2 * pair + 1):
+                for k, (src, dst) in zip((0, 3, 1), four_parts(j)):
+                    send(src, dst, a2a_send.at[j, k], a2a_recv.at[j, k], peers[j], sent)
 
     def from_peer(j, i, region):
         if j == 0:
@@ -270,17 +320,27 @@
 
         def first():
             for j in range(g * LANES // CAP, (g + 1) * LANES // CAP):
-                from_peer(j, 0, xt.at[rows_of(f), pl.ds(j * CAP, CAP)])
-                from_peer(j, 1, ct.at[rows_of(f), pl.ds(j * CAP, CAP)])
-            go(xt, rows_of(f), lanes, 0, at.across)
+                block = pl.ds(j * CAP, CAP)
+                from_peer(j, 1, ct.at[rows_of(f), block])
+                if g == 0:
+                    from_peer(j, 0, xt.at[rows_of(f), block])
+                else:
+                    from_peer(j, 0, xt.at[rows_of(at.x * 2, 2), block])
+                    from_peer(j, 3, xt.at[rows_of(at.x_far * 2, 2), block])
+            if g == 0:
+                go(xt, rows_of(f), lanes, 0, at.across)
             go(ct, rows_of(f), lanes, 6, at.right)
             go(ct, rows_of(f), lanes, 7, at.left)
             go(ct, rows_of(f), lanes, 5, at.across)
+            if g > 0:
+                go(xt, rows_of(at.x * 2, 2), lanes, 1, at.right)
+                go(xt, rows_of(at.x * 2, 2), lanes, 2, at.left)
 
         def second():
-            come(xt, rows_of(other), lanes, 0)
-            go(xt, rows_of(at.x * 2, 2), lanes, 1, at.right)
-            go(xt, rows_of(at.x * 2, 2), lanes, 2, at.left)
+            if g == 0:
+                come(xt, rows_of(other), lanes, 0)
+                go(xt, rows_of(at.x * 2, 2), lanes, 1, at.right)
+                go(xt, rows_of(at.x * 2, 2), lanes, 2, at.left)
             left, right = rows_of(at.x_left * 2 + zf), rows_of(at.x_right * 2 + zf)
             come(ct, left, lanes, 6)
             go(ct, left, halves[0], 8, at.right)
@@ -290,17 +350,22 @@
             go(ct, right, lanes, 11, at.across)
 
         def third():
-            come(xt, rows_of(at.x_left * 2, 2), lanes, 1)
-            go(xt, rows_of(at.x_left * 2), lanes, 3, at.right)
-            come(xt, rows_of(at.x_right * 2, 2), lanes, 2)
-            go(xt, rows_of(at.x_right * 2 + 1), lanes, 4, at.left)
+            if g == 0:
+                come(xt, rows_of(at.x_left * 2, 2), lanes, 1)
+                go(xt, rows_of(at.x_left * 2), lanes, 3, at.right)
+                come(xt, rows_of(at.x_right * 2, 2), lanes, 2)
+                go(xt, rows_of(at.x_right * 2 + 1), lanes, 4, at.left)
             for i in range(2):
                 come(ct, rows_of(far_slice), halves[i], 8 + i)
                 go(ct, rows_of(far_slice), halves[i], 12 + i, at.across)
 
         def fourth():
-            come(xt, rows_of(at.x_far * 2), lanes, 3)
-            come(xt, rows_of(at.x_far * 2 + 1), lanes, 4)
+            if g == 0:
+                come(xt, rows_of(at.x_far * 2), lanes, 3)
+                come(xt, rows_of(at.x_far * 2 + 1), lanes, 4)
+            else:
+                come(xt, rows_of(at.x_left * 2, 2), lanes, 1)
+                come(xt, rows_of(at.x_right * 2, 2), lanes, 2)
             come(ct, rows_of(other), lanes, 5)
             come(ct, rows_of(at.x_left * 2 + 1 - zf), lanes, 10)
             come(ct, rows_of(at.x_right * 2 + 1 - zf), lanes, 11)
@@ -387,11 +452,13 @@
             else:
                 grads_of[rows, :] += value
 
-    def reduce(g):
+    def reduce(g, along_x):
         a = g // (GROUPS // 2)
         zf = at.home(a) % 2
-        lanes_a = pl.ds(g * LANES, HALF)
-        lanes_b = pl.ds(g * LANES + HALF, HALF)
+        lanes_a = pl.ds(g * LANES, along_x)
+        along_z = LANES - along_x
+        lanes_b = pl.ds(g * LANES + along_x, along_z)
+        low, high = pl.ds(0, along_z // 2), pl.ds(along_z // 2, along_z // 2)
 
         def mine(x, z, lanes):
             return part.at[rows_of(x * 2 + z), lanes]
@@ -402,87 +469,84 @@
         def come(region, k):
             arrived(region, sum_send.at[g, k], sum_recv.at[g, k], at.across)
 
+        def view(buffer, i):
+            return buffer.at[g, i, :, pl.ds(0, along_x)]
+
+        def from_z(x):
+            return first_b.at[g, x, :, pl.ds(0, along_z)]
+
+        def from_x(i):
+            return second_b.at[g, i, :, low]
+
         def first():
+            if along_z:
+                for x in range(4):
+                    go(mine(x, 1 - zf, lanes_b), from_z(x), 8 + x, at.across)
+            if along_x:
+                go(mine(at.x_far, 0, lanes_a), view(first_a, 0), 0, at.right)
+                go(mine(at.x_far, 1, lanes_a), view(first_a, 1), 1, at.left)
+                go(mine(at.x_right, 1, lanes_a), view(second_a, 1), 2, at.right)
+                go(mine(at.x_left, 0, lanes_a), view(second_a, 2), 3, at.left)
+
+        def second():
+            if along_x:
+                come(view(first_a, 0), 0)
+                put(view(third_a, 0), view(first_a, 0)[...].astype(wide) + mine(at.x_right, 0, lanes_a)[...].astype(wide))
+                go(view(third_a, 0), view(second_a, 0), 4, at.right)
+                come(view(first_a, 1), 1)
+                put(view(third_a, 1), view(first_a, 1)[...].astype(wide) + mine(at.x_left, 1, lanes_a)[...].astype(wide))
+                go(view(third_a, 1), view(second_a, 3), 5, at.left)
+            if not along_z:
+                return
             for x in range(4):
-                go(mine(x, 1 - zf, lanes_b), first_b.at[g, x], 8 + x, at.across)
-            go(mine(at.x_far, 0, lanes_a), first_a.at[g, 0], 0, at.right)
-            go(mine(at.x_far, 1, lanes_a), first_a.at[g, 1], 1, at.left)
-            go(mine(at.x_right, 1, lanes_a), second_a.at[g, 1], 2, at.right)
-            go(mine(at.x_left, 0, lanes_a), second_a.at[g, 2], 3, at.left)
-
-        def second():
-            come(first_a.at[g, 0], 0)
-            put(
-                third_a.at[g, 0],
-                first_a[g, 0].astype(wide) + mine(at.x_right, 0, lanes_a)[...].astype(wide),
-            )
-            go(third_a.at[g, 0], second_a.at[g, 0], 4, at.right)
-            come(first_a.at[g, 1], 1)
-            put(
-                third_a.at[g, 1],
-                first_a[g, 1].astype(wide) + mine(at.x_left, 1, lanes_a)[...].astype(wide),
-            )
-            go(third_a.at[g, 1], second_a.at[g, 3], 5, at.left)
-            for x in range(4):
-                come(first_b.at[g, x], 8 + x)
+                come(from_z(x), 8 + x)
             for i, x in enumerate((at.x_far, at.x_right, at.x_left, at.x)):
                 put(
-                    mine_b.at[g, i],
-                    first_b[g, x].astype(wide) + mine(x, zf, lanes_b)[...].astype(wide),
+                    mine_b.at[g, i, :, pl.ds(0, along_z)],
+                    from_z(x)[...].astype(wide) + mine(x, zf, lanes_b)[...].astype(wide),
                 )
                 if i == 0:
-                    go(mine_b.at[g, 0, :, pl.ds(0, HALF // 2)], second_b.at[g, 0], 12, at.right)
-                    go(mine_b.at[g, 0, :, pl.ds(HALF // 2, HALF // 2)], second_b.at[g, 1], 13, at.left)
+                    go(mine_b.at[g, 0, :, low], from_x(0), 12, at.right)
+                    go(mine_b.at[g, 0, :, high], from_x(1), 13, at.left)
                 if i == 1:
-                    go(mine_b.at[g, 1, :, pl.ds(HALF // 2, HALF // 2)], second_b.at[g, 2], 14, at.right)
+                    go(mine_b.at[g, 1, :, high], from_x(2), 14, at.right)
                 if i == 2:
-                    go(mine_b.at[g, 2, :, pl.ds(0, HALF // 2)], second_b.at[g, 3], 15, at.left)
+                    go(mine_b.at[g, 2, :, low], from_x(3), 15, at.left)
 
         def third():
-            come(second_a.at[g, 0], 4)
-            come(second_a.at[g, 1], 2)
-            come(second_a.at[g, 2], 3)
-            come(second_a.at[g, 3], 5)
-            sums = [
-                second_a[g, z].astype(wide)
-                + second_a[g, 2 + z].astype(wide)
-                + mine(at.x, z, lanes_a)[...].astype(wide)
-                for z in range(2)
-            ]
-            keep = jnp.where(zf == 0, sums[0], sums[1])
-            give = jnp.where(zf == 0, sums[1], sums[0])
-            put(third_a.at[g, 2], give)
-            go(third_a.at[g, 2], third_a.at[g, 3], 6, at.across)
-            put(total.at[g, :, pl.ds(0, HALF)], keep)
-            come(second_b.at[g, 0], 12)
-            put(
-                second_b.at[g, 4],
-                second_b[g, 0].astype(wide) + mine_b[g, 1, :, pl.ds(0, HALF // 2)].astype(wide),
-            )
-            go(second_b.at[g, 4], second_b.at[g, 6], 16, at.right)
-            come(second_b.at[g, 1], 13)
-            put(
-                second_b.at[g, 5],
-                second_b[g, 1].astype(wide) + mine_b[g, 2, :, pl.ds(HALF // 2, HALF // 2)].astype(wide),
-            )
-            go(second_b.at[g, 5], second_b.at[g, 7], 17, at.left)
+            if along_x:
+                for i, k in enumerate((4, 2, 3, 5)):
+                    come(view(second_a, i), k)
+                sums_of = [
+                    view(second_a, z)[...].astype(wide)
+                    + view(second_a, 2 + z)[...].astype(wide)
+                    + mine(at.x, z, lanes_a)[...].astype(wide)
+                    for z in range(2)
+                ]
+                put(view(third_a, 2), jnp.where(zf == 0, sums_of[1], sums_of[0]))
+                go(view(third_a, 2), view(third_a, 3), 6, at.across)
+                put(total.at[g, :, pl.ds(0, along_x)], jnp.where(zf == 0, sums_of[0], sums_of[1]))
+            if not along_z:
+                return
+            come(from_x(0), 12)
+            put(from_x(4), from_x(0)[...].astype(wide) + mine_b[g, 1, :, low].astype(wide))
+            go(from_x(4), from_x(6), 16, at.right)
+            come(from_x(1), 13)
+            put(from_x(5), from_x(1)[...].astype(wide) + mine_b[g, 2, :, high].astype(wide))
+            go(from_x(5), from_x(7), 17, at.left)
 
         def fourth():
-            come(third_a.at[g, 3], 6)
-            put(
-                total.at[g, :, pl.ds(0, HALF)],
-                total[g, :, pl.ds(0, HALF)].astype(wide) + third_a[g, 3].astype(wide),
-            )
-            come(second_b.at[g, 6], 16)
-            come(second_b.at[g, 2], 14)
-            come(second_b.at[g, 3], 15)
-            come(second_b.at[g, 7], 17)
-            for i, (l, r) in enumerate(((6, 3), (2, 7))):
+            if along_x:
+                come(view(third_a, 3), 6)
+                region = total.at[g, :, pl.ds(0, along_x)]
+                put(region, region[...].astype(wide) + view(third_a, 3)[...].astype(wide))
+            for i, k in ((6, 16), (2, 14), (3, 15), (7, 17)):
+                if along_z:
+                    come(from_x(i), k)
+            for i, (l, r, cols) in enumerate(((6, 3, low), (2, 7, high)) if along_z else ()):
                 put(
-                    total.at[g, :, pl.ds(HALF + i * (HALF // 2), HALF // 2)],
-                    second_b[g, l].astype(wide)
-                    + second_b[g, r].astype(wide)
-                    + mine_b[g, 3, :, pl.ds(i * (HALF // 2), HALF // 2)].astype(wide),
+                    total.at[g, :, pl.ds(along_x + i * (along_z // 2), along_z // 2)],
+                    from_x(l)[...].astype(wide) + from_x(r)[...].astype(wide) + mine_b[g, 3, :, cols].astype(wide),
                 )
             for i in range(LANES // CAP):
                 j = g * (LANES // CAP) + i
@@ -528,34 +592,49 @@
         pltpu.make_async_copy(down_grads, down_out, local_sem.at[6]),
     ]
     spreads = [spread(g) for g in range(GROUPS)]
-    reduces = [reduce(g) for g in range(GROUPS)]
-    for tick in range(GROUPS + 6):
-        for k in range(4):
-            if 0 <= tick - k < GROUPS:
-                spreads[tick - k][k]()
-            if tick == 0 and k == 0:
-                for pair in range(2, N_BLK // 2):
-                    make_payload(pair)
-                spread_info()
-        done = tick - 3
-        if done == 0:
-            gather_info()
-        if 0 <= done < GROUPS:
-            forward(done)
-            reduces[done][0]()
-        for k in range(1, 4):
-            if 0 <= done - k < GROUPS:
-                reduces[done - k][k]()
-        if 0 <= done < GROUPS:
-            gates_of(done)
-            if done == GROUPS - 1:
-                gate_first()
-            weights(up_grads, pre_grad, xt, done)
-            weights(down_grads, act, hcot, done)
-            if done == GROUPS - 1:
-                for copy in results:
-                    copy.start()
-        if done == GROUPS + 1:
+    reduces = [reduce(g, along_x) for g, along_x in enumerate((HALF, LANES, HALF, HALF))]
+    def finish_group(g):
+        gates_of(g)
+        if g == GROUPS - 1:
+            gate_first()
+        weights(up_grads, pre_grad, xt, g)
+        weights(down_grads, act, hcot, g)
+
+    spreads[0][0]()
+    spread_info()
+    make_four()
+    make_four_payload(1)
+    make_four_payload(2)
+    spreads[0][1]()
+    spreads[1][0]()
+    make_four_payload(3)
+    spreads[0][2]()
+    spreads[1][1]()
+    spreads[2][0]()
+    spreads[0][3]()
+    gather_info()
+    forward(0)
+    reduces[0][0]()
+    spreads[2][1]()
+    spreads[1][2]()
+    spreads[3][0]()
+    finish_group(0)
+    for g in range(1, GROUPS + 3):
+        for k in (1, 2, 3):
+            if g + 3 - k < GROUPS:
+                spreads[g + 3 - k][k]()
+        if g < GROUPS:
+            forward(g)
+            reduces[g][0]()
+        for k in (1, 2, 3):
+            if 0 <= g - k < GROUPS:
+                reduces[g - k][k]()
+        if g < GROUPS:
+            finish_group(g)
+        if g == GROUPS - 1:
+            for copy in results:
+                copy.start()
+        if g == GROUPS + 1:
             gate_second()
 
     for j in range(N_BLK):
@@ -569,7 +648,7 @@
 
     mixed = dot(back[...], chosen[...])
     scale = jnp.concatenate(
-        [jnp.broadcast_to(1.0 + columns[1, :, b : b + 1], (NARROW, PATCHES)) for b in range(2)], axis=1
+        [jnp.broadcast_to(1.0 + columns[:, 2 + b : 3 + b], (NARROW, PATCHES)) for b in range(2)], axis=1
     )
     norm_grad = mixed * scale
     sums[0:1, :] = jnp.sum(norm_grad, axis=0, keepdims=True)
@@ -682,8 +761,12 @@
         scratch_shapes=[
             pltpu.VMEM((SLOTS, TOKENS), bf16),
             pltpu.VMEM((2 * NARROW, 2 * TOKENS), bf16),
+            pltpu.VMEM((5 * NARROW, 2 * TOKENS), bf16),
+            pltpu.VMEM((4 * NARROW, TOKENS), f32),
+            pltpu.VMEM((4, NARROW, 128), f32),
             pltpu.VMEM((8, 2 * TOKENS), jnp.int32),
-            pltpu.VMEM((2 * NARROW, SLOTS), bf16),
+            pltpu.VMEM((2 * NARROW, LANES), bf16),
+            pltpu.VMEM((5 * NARROW, SLOTS - LANES), bf16),
             pltpu.VMEM((NARROW, SLOTS), bf16),
             pltpu.VMEM((N_BLK, 2, 256), f32),
             pltpu.VMEM((2, TOKENS), f32),
@@ -702,9 +785,9 @@
             pltpu.VMEM((width, 128), bf16),
             pltpu.VMEM((8 * N_BLK, 128), f32),
             pltpu.VMEM((N_HID, 2 * N_BLK, 256), f32),
-            pltpu.VMEM((GROUPS, 2, NARROW, HALF), bf16),
-            pltpu.VMEM((GROUPS, 4, NARROW, HALF), bf16),
-            pltpu.VMEM((GROUPS, 4, NARROW, HALF), bf16),
+            pltpu.VMEM((GROUPS, 2, NARROW, LANES), bf16),
+            pltpu.VMEM((GROUPS, 4, NARROW, LANES), bf16),
+            pltpu.VMEM((GROUPS, 4, NARROW, LANES), bf16),
             pltpu.VMEM((GROUPS, 4, NARROW, HALF), bf16),
             pltpu.VMEM((GROUPS, 8, NARROW, HALF // 2), bf16),
             pltpu.VMEM((GROUPS, 4, NARROW, HALF), bf16),
@@ -712,8 +795,8 @@
             pltpu.VMEM((N_HID, 2 * N_BLK, 256), f32),
             pltpu.VMEM((2 * N_BLK, 256), f32),
             pltpu.VMEM((N_BLK, 2, 256), f32),
-            dma((N_BLK, 3)),
-            dma((N_BLK, 3)),
+            dma((N_BLK, 4)),
+            dma((N_BLK, 4)),
             dma((GROUPS, 14)),
             dma((GROUPS, 14)),
             dma((N_HID,)),
@@ -726,6 +809,8 @@
             dma((N_HID,)),
             dma((N_BLK + N_HID,)),
             dma((N_BLK + N_HID,)),
+            dma((3,)),
+            dma((3,)),
             dma((7,)),
         ],
         compiler_params=pltpu.CompilerParams(

time: 152 us -> 142 us (0.934)
  Pallas kernels: 151 us -> 141 us
    pallas_call x1, Pallas kernels: 140 us -> 130 us  [run_experts(): pl.pallas_call(expert_kernel, out_shape=(jax.ShapeDtypeStruct((NARROW, TO...]
where the time goes in v5:
time: 142 us
  Pallas kernels  141 us (99%)
    pallas_call x1, Pallas kernels, run_experts(): pl.pallas_call(expert_kernel, out_shape=(jax.ShapeDtypeStruct((NARROW, TO...  130 us
    pallas_call x1, Pallas kernels, results_of(): pl.pallas_call(result_kernel, out_shape=(jax.ShapeDtypeStruct((NARROW, TO...  6.66 us
    pallas_call x1, Pallas kernels, modulation(): pl.pallas_call(modulation_kernel, out_shape=(jax.ShapeDtypeStruct((NARROW...  3.71 us

profile of v5, /device:TPU:1, one launch (start us, length us, event | category | flops | bytes accessed | tf_op | source)
XLA Modules:
  0.0 141.7 jit_solution(666915634142565939)
XLA Ops:
  0.6 3.7 %shard_map.137 = (f32[144,128]{1,0:T(8,128)}, f32[16,8,256]{2,1,0:T(8,128)}) custom-call(s32[2]{0:T(128)} %steps.1, f32[1000,1152]{1,0:T(8,128)} %table.1, f32[432,1152]{1,0:T(8,128)} %bitcast.16, f32[3,144]{1,0:T(4,128)} %bias.1, s32[2,512]{1,0:T(2,128)} %bitcast.21), custom_call_target="tpu_custom_call" | custom-call | tf_op jit(solution)/shard_map/pallas_call | solution.py:143
  4.3 130.5 %shard_map.138 = (f32[144,512]{1,0:T(8,128)}, f32[144,512]{1,0:T(8,128)}, f32[8,512]{1,0:T(8,128)}, f32[2,512]{1,0:T(2,128)}, f32[16,8,256]{2,1,0:T(8,128)}, /*i...) custom-call(bf16[512,1152]{1,0:T(8,128)(2,1)} %tokens.1, bf16[144,512]{1,0:T(8,128)(2,1)} %bitcast.19, ...), custom_call_target="tpu_custom_call" | custom-call | tf_op jit(solution)/shard_map/pallas_call | solution.py:747
  134.8 6.7 %shard_map.139 = (bf16[144,512]{1,0:T(8,128)(2,1)}, f32[576,1152]{1,0:T(8,128)}, f32[576,1152]{1,0:T(8,128)}, f32[3,72,144]{2,1,0:T(8,128)}, f32[3,144]{1,0:T(4,128)}) custom-call(bf16[144,512]{1,0:T(8,128)(2,1)} %bitcast.20, f32[144,512]{1,0:T(8,128)} %get-tuple-element.22.norm_grads, f32[144,512]{1,0:T(8,128)} %get-tuple-element.23.normed, ...), custom_call_target="tpu_custom_call" | custom-call | tf_op jit(solution)/shard_map/pallas_call | solution.py:726

commit v6 on v5

--- a/solution.py
+++ b/solution.py
@@ -402,7 +402,7 @@
         hit = (row // 8 == block) & (is_first == (row % 2 == 0)) & (row % 8 < 6)
         return jnp.where(hit, 1.0, 0.0).astype(bf16)
 
-    def forward(g):
+    def forward(g, pair_ready):
         lanes = pl.ds(g * LANES, LANES)
         images = image_of_lane(g)
 
@@ -419,10 +419,10 @@
             act[rows, :] = activated.astype(bf16)
             pre_grad[rows, :] = (dot(down[rows, :], hcot[:, lanes]) * slope).astype(bf16)
 
-        @pl.loop(0, 4)
-        def _(i):
+        for i in range(4):
             rows = rows_of(2 * i, 2)
             part[rows, lanes] = dot(up[rows, :], pre_grad[...]).astype(bf16)
+            pair_ready(i)
 
     def gates_of(g):
         lanes = pl.ds(g * LANES, LANES)
@@ -478,10 +478,11 @@
         def from_x(i):
             return second_b.at[g, i, :, low]
 
+        def pair_ready(x):
+            if along_z:
+                go(mine(x, 1 - zf, lanes_b), from_z(x), 8 + x, at.across)
+
         def first():
-            if along_z:
-                for x in range(4):
-                    go(mine(x, 1 - zf, lanes_b), from_z(x), 8 + x, at.across)
             if along_x:
                 go(mine(at.x_far, 0, lanes_a), view(first_a, 0), 0, at.right)
                 go(mine(at.x_far, 1, lanes_a), view(first_a, 1), 1, at.left)
@@ -557,7 +558,7 @@
                 else:
                     send(src, dst, back_send.at[j, 0], back_recv.at[j, 0], owners[j], sent)
 
-        return first, second, third, fourth
+        return first, second, third, fourth, pair_ready
 
     def gate_first():
         for i in range(1, N_HID):
@@ -613,7 +614,7 @@
     spreads[2][0]()
     spreads[0][3]()
     gather_info()
-    forward(0)
+    forward(0, reduces[0][4])
     reduces[0][0]()
     spreads[2][1]()
     spreads[1][2]()
@@ -624,7 +625,7 @@
             if g + 3 - k < GROUPS:
                 spreads[g + 3 - k][k]()
         if g < GROUPS:
-            forward(g)
+            forward(g, reduces[g][4])
             reduces[g][0]()
         for k in (1, 2, 3):
             if 0 <= g - k < GROUPS:
@@ -689,10 +690,10 @@
     token_grads, up_grads, down_grads, weight_grads, bias_grads, held, move_sem,
 ):
     f32 = jnp.float32
-    share = up_in.shape[0] // 4
+    share = up_in.shape[0] // 2
     loads, stores = [], []
     for i, (src, dst) in enumerate(((up_in, up_grads), (down_in, down_grads))):
-        for k in range(4):
+        for k in range(2):
             rows = pl.ds(k * share, share)
             loads.append(pltpu.make_async_copy(src.at[rows], held.at[i, rows], move_sem.at[0, i, k]))
             stores.append(pltpu.make_async_copy(held.at[i, rows], dst.at[rows], move_sem.at[1, i, k]))
@@ -734,7 +735,7 @@
         ),
         in_specs=[vmem] * 7 + [anywhere] * 2,
         out_specs=[vmem, anywhere, anywhere, vmem, vmem],
-        scratch_shapes=[pltpu.VMEM((2, hidden, width), f32), pltpu.SemaphoreType.DMA((2, 2, 4))],
+        scratch_shapes=[pltpu.VMEM((2, hidden, width), f32), pltpu.SemaphoreType.DMA((2, 2, 2))],
         compiler_params=pltpu.CompilerParams(vmem_limit_bytes=60 * 2**20),
     )(*operands)
 

time: 142 us -> 140 us (0.986)
  Pallas kernels: 141 us -> 139 us
    pallas_call x1, Pallas kernels: 130 us -> 129 us  [run_experts(): pl.pallas_call(expert_kernel, out_shape=(jax.ShapeDtypeStruct((NARROW, TO...]
where the time goes in v6:
time: 140 us
  Pallas kernels  139 us (99%)
    pallas_call x1, Pallas kernels, run_experts(): pl.pallas_call(expert_kernel, out_shape=(jax.ShapeDtypeStruct((NARROW, TO...  129 us
    pallas_call x1, Pallas kernels, results_of(): pl.pallas_call(result_kernel, out_shape=(jax.ShapeDtypeStruct((NARROW, TO...  6.27 us
    pallas_call x1, Pallas kernels, modulation(): pl.pallas_call(modulation_kernel, out_shape=(jax.ShapeDtypeStruct((NARROW...  3.71 us

profile of v6, /device:TPU:1, one launch (start us, length us, event | category | flops | bytes accessed | tf_op | source)
XLA Modules:
  0.0 139.8 jit_solution(1200273301068847123)
XLA Ops:
  0.6 3.7 %shard_map.137 = (f32[144,128]{1,0:T(8,128)}, f32[16,8,256]{2,1,0:T(8,128)}) custom-call(s32[2]{0:T(128)} %steps.1, f32[1000,1152]{1,0:T(8,128)} %table.1, f32[432,1152]{1,0:T(8,128)} %bitcast.16, f32[3,144]{1,0:T(4,128)} %bias.1, s32[2,512]{1,0:T(2,128)} %bitcast.21), custom_call_target="tpu_custom_call" | custom-call | tf_op jit(solution)/shard_map/pallas_call | solution.py:143
  4.3 129.0 %shard_map.138 = (f32[144,512]{1,0:T(8,128)}, f32[144,512]{1,0:T(8,128)}, f32[8,512]{1,0:T(8,128)}, f32[2,512]{1,0:T(2,128)}, f32[16,8,256]{2,1,0:T(8,128)}, /*i...) custom-call(bf16[512,1152]{1,0:T(8,128)(2,1)} %tokens.1, bf16[144,512]{1,0:T(8,128)(2,1)} %bitcast.19, ...), custom_call_target="tpu_custom_call" | custom-call | tf_op jit(solution)/shard_map/pallas_call | solution.py:748
  133.3 6.3 %shard_map.139 = (bf16[144,512]{1,0:T(8,128)(2,1)}, f32[576,1152]{1,0:T(8,128)}, f32[576,1152]{1,0:T(8,128)}, f32[3,72,144]{2,1,0:T(8,128)}, f32[3,144]{1,0:T(4,128)}) custom-call(bf16[144,512]{1,0:T(8,128)(2,1)} %bitcast.20, f32[144,512]{1,0:T(8,128)} %get-tuple-element.22.norm_grads, f32[144,512]{1,0:T(8,128)} %get-tuple-element.23.normed, ...), custom_call_target="tpu_custom_call" | custom-call | tf_op jit(solution)/shard_map/pallas_call | solution.py:727
